TPU v7x, 256 devices: a whole 4x4x8 slice. The times are simulated.
256 devices in a mesh: gx: 32 (over y_lo, z, core), gy: 8 (over x, y_hi).
Axes of the slice: x: 4, y: 4 (y_hi: 2, y_lo: 2; y = y_hi * 2 + y_lo), z: 8, core: 2. Of those that a mesh axis runs over, the one named last changes fastest.
Arguments:
- eigen_vecs: bfloat16 [2, 3, 4, 128, 128, 512], P(None, None, None, 'gx', 'gy'), may hold values from -6 to 6
- gauge_links: float32 [2, 2, 3, 3, 4, 128, 128], P(None, None, None, None, None, 'gx', 'gy'), may hold values from -4 to 4
- directions: int32 [4], replicated, may hold values from 0 to 3, each once
- spin_map: int32 [4], replicated, may hold values from 0 to 3, each once
- perambulator: bfloat16 [2, 2048, 2048], P(None, ('gx', 'gy')), may hold values from -0.125 to 0.125
Outputs:
- elementals: float32 [4, 2, 512, 512], P(None, None, 'gx')
- contracted: bfloat16 [4, 2, 2048, 2048], P(None, None, ('gx', 'gy'))
Inputs may be any that keep to these rules, and one draw needn't show every extreme that they name: `directions`: a permutation of the four hops: 0 and 1 are forward hops along x and y, 2 and 3 backward hops along x and y. `spin_map`: a permutation of the four spins.
All inputs are finite; a program needn't handle non-finite values.
Results may differ from a plain program's by a relative error of at most 0.0058.
Values may be sent and summed in bfloat16 or wider, within the bound.
A program may use at most 128 MiB of HBM per device.

v0:
```python
import math

import jax
import jax.numpy as jnp
from jax import lax
from jax.sharding import PartitionSpec as P


def with_halo(block, sides, width):
    for axis, dim in sides:
        count = lax.axis_size(axis)
        forward = [(i, i + 1) for i in range(count - 1)]
        forward.append((count - 1, 0))
        backward = [(target, source) for source, target in forward]
        low = lax.ppermute(
            lax.slice_in_dim(block, block.shape[dim] - width, None, axis=dim), axis, forward
        )
        high = lax.ppermute(lax.slice_in_dim(block, 0, width, axis=dim), axis, backward)
        block = jnp.concatenate([low, block, high], axis=dim)
    return block


def colour_apply(gauge_link, colour_field, dagger):
    values = colour_field.astype(jnp.float32)
    rows_re = []
    rows_im = []
    for row in range(3):
        acc_re = jnp.zeros(values.shape[2:], jnp.float32)
        acc_im = jnp.zeros(values.shape[2:], jnp.float32)
        for column in range(3):
            if dagger:
                coef_re = gauge_link[0, column, row][..., None]
                coef_im = -gauge_link[1, column, row][..., None]
            else:
                coef_re = gauge_link[0, row, column][..., None]
                coef_im = gauge_link[1, row, column][..., None]
            acc_re = acc_re + coef_re * values[0, column] - coef_im * values[1, column]
            acc_im = acc_im + coef_re * values[1, column] + coef_im * values[0, column]
        rows_re.append(acc_re)
        rows_im.append(acc_im)
    return jnp.stack([jnp.stack(rows_re, 0), jnp.stack(rows_im, 0)], 0)


def gram_term(field, displaced):
    count = field.shape[-1]
    left_re = field[0].reshape(-1, count)
    left_im = field[1].reshape(-1, count)
    right_re = displaced[0].reshape(-1, count)
    right_im = displaced[1].reshape(-1, count)
    real = jnp.dot(left_re.T, right_re, preferred_element_type=jnp.float32) + jnp.dot(
        left_im.T, right_im, preferred_element_type=jnp.float32
    )
    imag = jnp.dot(left_re.T, right_im, preferred_element_type=jnp.float32) - jnp.dot(
        left_im.T, right_re, preferred_element_type=jnp.float32
    )
    return jnp.stack([real, imag], 0)


def make_source(eigen_vecs, gauge_links, heading):
    hop_axis = heading % 2
    chosen_link = lax.dynamic_index_in_dim(gauge_links, hop_axis, axis=0, keepdims=False)
    return lax.cond(
        heading < 2,
        lambda: eigen_vecs,
        lambda: colour_apply(chosen_link, eigen_vecs, True).astype(jnp.bfloat16),
    )


def displace(padded, gauge_links, heading):

    def forward_x():
        return colour_apply(gauge_links[0], padded[:, :, :, 2:, 1:-1], False).astype(jnp.bfloat16)

    def forward_y():
        return colour_apply(gauge_links[1], padded[:, :, :, 1:-1, 2:], False).astype(jnp.bfloat16)

    def backward_x():
        return padded[:, :, :, :-2, 1:-1]

    def backward_y():
        return padded[:, :, :, 1:-1, :-2]

    return lax.switch(heading, [forward_x, forward_y, backward_x, backward_y])


def add_pieces(left_re, left_im, running, pieces):
    row_count = pieces.shape[2]
    lhs_block = jnp.concatenate(
        [
            lax.slice_in_dim(left_re, 0, row_count, axis=1),
            lax.slice_in_dim(left_im, 0, row_count, axis=1),
        ],
        axis=1,
    )
    updated = []
    for disp_index in range(pieces.shape[0]):
        part_re = pieces[disp_index, 0]
        part_im = pieces[disp_index, 1]
        rhs_block = jnp.concatenate(
            [jnp.concatenate([part_re, part_im], 1), jnp.concatenate([-part_im, part_re], 1)], 0
        )
        updated.append(
            running[disp_index] + jnp.dot(lhs_block, rhs_block, preferred_element_type=jnp.float32)
        )
    return jnp.stack(updated, 0)


def local(eigen_vecs, gauge_links, directions, spin_map, perambulator):
    vec_count = eigen_vecs.shape[-1]
    disp_count = directions.shape[0]
    site_total = (
        eigen_vecs.shape[2]
        * eigen_vecs.shape[3]
        * eigen_vecs.shape[4]
        * lax.axis_size("gx")
        * lax.axis_size("gy")
    )
    norm_factor = 1.0 / math.sqrt(3.0 * site_total)
    source_list = [
        make_source(eigen_vecs, gauge_links, directions[disp_index])
        for disp_index in range(disp_count)
    ]
    displaced_list = []
    sources = jnp.stack(source_list, axis=0)
    padded = with_halo(sources, (("gx", 4), ("gy", 5)), 1)
    for disp_index in range(disp_count):
        displaced_list.append(displace(padded[disp_index], gauge_links, directions[disp_index]))
    gram_terms = [
        gram_term(eigen_vecs, displaced_list[disp_index]) for disp_index in range(disp_count)
    ]
    partial_value = jnp.stack(gram_terms, 0) * norm_factor
    row_total = perambulator.shape[1]
    blocks = perambulator.reshape(2, row_total, 4, vec_count)
    onehot = (spin_map[:, None] == jnp.arange(4, dtype=jnp.int32)[None, :]).astype(jnp.bfloat16)
    chosen = jnp.einsum("prtn,st->prsn", blocks, onehot, preferred_element_type=jnp.float32).astype(
        jnp.bfloat16
    )
    left_re = chosen[0].reshape(row_total * 4, vec_count)
    left_im = chosen[1].reshape(row_total * 4, vec_count)
    zero_init = jnp.zeros((disp_count, row_total * 4, 2 * vec_count), jnp.float32)
    share_rows = vec_count // lax.axis_size("gx")
    summed_all = lax.psum(partial_value, ("gx", "gy"))
    own_rows = lax.dynamic_slice_in_dim(
        summed_all, lax.axis_index("gx") * share_rows, share_rows, 2
    )
    product = add_pieces(left_re, left_im, zero_init, summed_all.astype(jnp.bfloat16))
    contracted = (
        product.reshape(disp_count, row_total, 4, 2, vec_count)
        .transpose(0, 3, 1, 2, 4)
        .reshape(disp_count, 2, row_total, 4 * vec_count)
    )
    return (own_rows, contracted.astype(jnp.bfloat16))


def solution(mesh):
    in_specs = (
        P(None, None, None, "gx", "gy", None),
        P(None, None, None, None, None, "gx", "gy"),
        P(),
        P(),
        P(None, ("gx", "gy"), None),
    )
    out_specs = (P(None, None, "gx", None), P(None, None, ("gx", "gy"), None))
    return jax.shard_map(local, mesh=mesh, in_specs=in_specs, out_specs=out_specs, check_vma=False)
```

profile of v0, /device:TPU:1, one launch (start us, length us, event | category | flops | bytes accessed | tf_op | source)
XLA Modules:
  0.0 475.4 jit_solution(6210702405623555138)
XLA Ops:
  7.2 1.4 fusion.143
  18.5 6.2 %conditional.8 = (bf16[1,2,3,4,4,16,512]{6,3,5,4,2,1,0:T(4,128)(2,1)S(1)}) conditional(s32[]{:T(128)} %convert_element_type.113, (f32[2,2,3,3,4,4,16]{6,5,4,3,2,1,0:T(4,128)}, bf16[2,3,4,4,16,512]{5,4,3,2,1,0:T(8,128)(2,1)}, s32[]{:T(128)}, s32[]{:T(128)}, s32[]{:T(128)}, /*index=5*/s32[]{:T(128)}, s32[]{:T(128)}) %tuple.161, ...), branch_computations={%region_0.1_spmd.clone, %region_1.2_spmd} | conditional | flops 12585219 | bytes 25258030 | solution.py:62
  18.6 0.9 dynamic-slice_bitcast_fusion
  19.5 1.9 convert_element_type.122
  23.3 1.4 copy.50
  24.7 1.8 constant_dynamic-update-slice_fusion.3
  26.6 1.4 conditional.9
  26.6 1.4 copy.53
  28.0 1.9 constant_dynamic-update-slice_fusion.2
  29.9 1.7 conditional.10
  30.1 1.4 copy.55
  31.6 1.9 constant_dynamic-update-slice_fusion.1
  33.5 13.6 %conditional.11 = (bf16[1,2,3,4,4,16,512]{6,3,5,4,2,1,0:T(4,128)(2,1)S(1)}) conditional(s32[]{:T(128)} %convert_element_type.116, (f32[2,2,3,3,4,4,16]{6,5,4,3,2,1,0:T(4,128)S(1)}, bf16[2,3,4,4,16,512]{5,4,3,2,1,0:T(8,128)(2,1)S(1)}, s32[]{:T(128)}, s32[]{:T(128)}, s32[]{:T(128)}, /*index=5*/s32[]{:T(128)}, s32[]{:T(128)}) %tuple.527, ...), branch_computations={%region_6.7_spmd.clone, %region_7.8_spmd} | conditional | flops 12585219 | bytes 25258030 | solution.py:62
  35.8 1.4 copy.56
  47.0 1.8 constant_dynamic-update-slice_fusion
  48.9 4.2 fusion.141
  53.0 3.1 collective-permute-start
  56.4 17.1 %collective-permute-done = bf16[4,2,3,4,1,16,512]{6,3,5,4,2,1,0:T(4,128)(2,1)S(1)} collective-permute-done((bf16[4,2,3,4,1,16,512]{6,3,5,4,2,1,0:T(4,128)(2,1)S(1)}, bf16[4,2,3,4,1,16,512]{6,3,5,4,2,1,0:T(4,128)(2,1)S(1)}, u32[]{:S(2)}, u32[]{:S(2)}) %collective-permute-start) | collective-permute-done | bytes 1572896 | tf_op jit(solution)/shard_map/ppermute | solution.py:15
  73.5 2.8 collective-permute-done.1
  76.3 1.8 pad_maximum_fusion.23
  78.1 2.9 collective-permute-start.2
  81.1 2.2 collective-permute-start.3
  85.7 19.4 %collective-permute-done.2 = bf16[4,2,3,4,6,1,512]{6,3,5,4,2,1,0:T(4,128)(2,1)} collective-permute-done((bf16[4,2,3,4,6,1,512]{6,3,5,4,2,1,0:T(4,128)(2,1)}, bf16[4,2,3,4,6,1,512]{6,3,5,4,2,1,0:T(4,128)(2,1)}, u32[]{:S(2)}, u32[]{:S(2)}) %collective-permute-start.2) | collective-permute-done | bytes 589856 | tf_op jit(solution)/shard_map/ppermute | solution.py:15
  105.1 4.9 %collective-permute-done.3 = bf16[4,2,3,4,6,1,512]{6,3,5,4,2,1,0:T(4,128)(2,1)} collective-permute-done((bf16[4,2,3,4,6,1,512]{6,3,5,4,2,1,0:T(4,128)(2,1)}, bf16[4,2,3,4,6,1,512]{6,3,5,4,2,1,0:T(4,128)(2,1)}, u32[]{:S(2)}, u32[]{:S(2)}) %collective-permute-start.3) | collective-permute-done | bytes 589856 | tf_op jit(solution)/shard_map/ppermute | solution.py:18
  110.0 10.9 %pad_maximum_fusion.20 = bf16[4,2,3,4,6,18,512]{6,3,5,4,2,1,0:T(4,128)(2,1)S(1)} fusion(bf16[4,2,3,4,6,1,512]{6,3,5,4,2,1,0:T(4,128)(2,1)} %collective-permute-done.3, bf16[4,2,3,4,1,16,512]{6,3,5,4,2,1,0:T(4,128)(2,1)} %copy-done.7, bf16[4,2,3,4,4,16,512]{6,3,5,4,2,1,0:T(4,128)(2,1)} %constant_dynamic-update-slice_fusion, ...), kind=kLoop, calls=%fused_computation.460 | loop fusion | flops 21233664 | bytes 21233664 | tf_op jit(solution)/shard_map/concatenate | solution.py:19
  120.9 5.7 %slice_bitcast_fusion.279 = (bf16[2,3,4,6,18,512]{5,2,4,3,1,0:T(4,128)(2,1)}, bf16[2,3,4,6,18,512]{5,2,4,3,1,0:T(4,128)(2,1)}, bf16[2,3,4,6,18,512]{5,2,4,3,1,0:T(4,128)(2,1)}, bf16[2,3,4,6,18,512]{5,2,4,3,1,0:T(4,128)(2,1)S(1)}) fusion(bf16[4,2,3,4,6,18,512]{6,3,5,4,2,1,0:T(4,128)(2,1)S(1)} %pad_maximum_fusion.20), kind=kLoop, calls=%fused_computation.465 | loop fusion | bytes 21233664 | tf_op jit(solution)/shard_map/squeeze | solution.py:127
  126.5 3.6 conditional.13
  126.6 0.8 copy.18
  131.8 1.9 fusion.73
  134.0 1.6 fusion.75
  135.6 6.1 %conditional.12 = ((bf16[3,4,4,16,512]{4,3,2,1,0:T(8,128)(2,1)}, bf16[3,4,4,16,512]{4,3,2,1,0:T(8,128)(2,1)})) conditional(s32[]{:T(128)} %clamp.12, (f32[2,2,3,3,4,4,16]{6,5,4,3,2,1,0:T(4,128)S(1)}, bf16[2,3,4,6,18,512]{5,2,4,3,1,0:T(4,128)(2,1)S(1)}) %tuple.530, (f32[2,2,3,3,4,4,16]{6,5,4,3,2,1,0:T(4,128)S(1)}, ...), branch_computations={%region_8.9_spmd, %region_9.10_spmd, %region_10.11_spmd, %region_1... | conditional | flops 11796480 | bytes 24274952 | solution.py:83
  135.6 0.8 copy.58
  136.4 2.1 slice_bitcast_fusion.50
  141.7 1.8 convolution_bitcast_fusion.14
  143.5 0.6 convolution_bitcast_fusion.12
  144.1 1.6 fusion.69
  146.4 1.6 fusion.71
  148.1 2.2 conditional.15
  148.1 0.8 copy.65
  148.9 1.4 slice_bitcast_fusion.214
  150.3 1.8 convolution_bitcast_fusion.2
  152.1 0.6 convolution_bitcast_fusion
  152.7 1.6 fusion.81
  155.0 1.6 fusion.83
  156.6 4.5 conditional.14
  156.6 0.8 copy.23
  159.5 1.3 pad_maximum_fusion.10
  161.1 1.8 convolution_bitcast_fusion.6
  162.9 0.6 convolution_bitcast_fusion.4
  163.5 0.6 fusion.77
  165.2 0.6 copy-done.8
  166.9 0.8 copy-done.11
  168.6 4.1 maximum_multiply_fusion
  172.7 0.6 copy-done.23
  173.7 276.2 %all-reduce.2.cloned.1.call-done = f32[4,2,512,512]{2,3,1,0:T(8,128)} async-done(((f32[4,2,512,512]{2,3,1,0:T(8,128)}), f32[4,2,512,512]{2,3,1,0:T(8,128)}) %all-reduce.2.cloned.1.call-update) | async-done | bytes 8388624 | tf_op jit(solution)/shard_map/psum | solution.py:142
  449.9 3.9 convert_element_type.119
  454.1 1.2 fusion.137
  455.3 0.7 fusion.93
  456.1 1.7 fusion.90
  457.9 1.8 fusion.87
  459.8 0.7 fusion.84
  461.0 0.8 copy.31
  461.8 3.5 constant_dynamic-slice_fusion
  465.3 2.9 copy.32
  (92 shorter events, 16.7 us)
Async XLA Ops:
  7.2 165.6 %copy-start = (bf16[2,8,2048]{2,1,0:T(8,128)(2,1)S(1)}, bf16[2,8,2048]{2,1,0:T(8,128)(2,1)}, u32[]{:S(2)}) copy-start(bf16[2,8,2048]{2,1,0:T(8,128)(2,1)} %param.33) | copy-start | bytes 196612
  7.2 442.7 %all-reduce.2.cloned.1.call-start = ((), (), s32[]{:S(2)}) async-start(), calls=%async_computation | async-start | bytes 16777216 | tf_op jit(solution)/shard_map/psum | solution.py:142
  24.7 1.9 copy-start.1
  24.7 1.9 copy-start.6
  48.9 27.4 %copy-start.5 = (bf16[4,2,3,4,4,16,512]{6,3,5,4,2,1,0:T(4,128)(2,1)S(1)}, bf16[4,2,3,4,4,16,512]{6,3,5,4,2,1,0:T(4,128)(2,1)}, u32[]{:S(2)}) copy-start(bf16[4,2,3,4,4,16,512]{6,3,5,4,2,1,0:T(4,128)(2,1)} %constant_dynamic-update-slice_fusion) | copy-start | bytes 18874372
  53.0 20.5 %collective-permute-start = (bf16[4,2,3,4,1,16,512]{6,3,5,4,2,1,0:T(4,128)(2,1)S(1)}, bf16[4,2,3,4,1,16,512]{6,3,5,4,2,1,0:T(4,128)(2,1)S(1)}, u32[]{:S(2)}, u32[]{:S(2)}) collective-permute-start(bf16[4,2,3,4,1,16,512]{6,3,5,4,2,1,0:T(4,128)(2,1)S(1)} %get-tuple-element.668), channel_id=1, source_target_pairs={{0,8},{8,16},{16,24},{24,32},{32,40},{40,48},{48,56},{56,64},{64,7... | collective-permute-start | bytes 4718600 | tf_op jit(solution)/shard_map/ppermute | solution.py:15
  56.1 20.1 %collective-permute-start.1 = (bf16[4,2,3,4,1,16,512]{6,3,5,4,2,1,0:T(4,128)(2,1)S(1)}, bf16[4,2,3,4,1,16,512]{6,3,5,4,2,1,0:T(4,128)(2,1)S(1)}, u32[]{:S(2)}, u32[]{:S(2)}) collective-permute-start(bf16[4,2,3,4,1,16,512]{6,3,5,4,2,1,0:T(4,128)(2,1)S(1)} %get-tuple-element.669), channel_id=1, source_target_pairs={{8,0},{16,8},{24,16},{32,24},{40,32},{48,40},{56,48},{64,56},{72,6... | collective-permute-start | bytes 4718600 | tf_op jit(solution)/shard_map/ppermute | solution.py:18
  76.3 1.9 copy-start.7
  78.1 27.0 %collective-permute-start.2 = (bf16[4,2,3,4,6,1,512]{6,3,5,4,2,1,0:T(4,128)(2,1)}, bf16[4,2,3,4,6,1,512]{6,3,5,4,2,1,0:T(4,128)(2,1)}, u32[]{:S(2)}, u32[]{:S(2)}) collective-permute-start(bf16[4,2,3,4,6,1,512]{6,3,5,4,2,1,0:T(4,128)(2,1)} %get-tuple-element.666), channel_id=1, source_target_pairs={{0,1},{1,2},{2,3},{3,4},{4,5},{5,6},{6,7},{7,0},{8,9},{9,10},{10,1... | collective-permute-start | bytes 1769480 | tf_op jit(solution)/shard_map/ppermute | solution.py:15
  81.1 28.9 %collective-permute-start.3 = (bf16[4,2,3,4,6,1,512]{6,3,5,4,2,1,0:T(4,128)(2,1)}, bf16[4,2,3,4,6,1,512]{6,3,5,4,2,1,0:T(4,128)(2,1)}, u32[]{:S(2)}, u32[]{:S(2)}) collective-permute-start(bf16[4,2,3,4,6,1,512]{6,3,5,4,2,1,0:T(4,128)(2,1)} %get-tuple-element.667), channel_id=1, source_target_pairs={{1,0},{2,1},{3,2},{4,3},{5,4},{6,5},{7,6},{0,7},{9,8},{10,9},{11,1... | collective-permute-start | bytes 1769480 | tf_op jit(solution)/shard_map/ppermute | solution.py:18
  130.1 0.9 copy-start.14
  130.1 1.1 copy-start.13
  131.8 2.0 copy-start.4
  131.8 2.2 copy-start.15
  141.7 1.8 copy-start.16
  144.1 2.1 copy-start.3
  144.1 2.3 copy-start.17
  150.3 1.8 copy-start.18
  152.7 2.1 copy-start.2
  152.7 2.3 copy-start.19
  161.1 1.8 copy-start.20
  163.5 1.1 copy-start.21
  164.6 1.2 copy-start.8
  164.6 1.5 copy-start.9
  164.6 1.9 copy-start.10
  166.5 1.2 copy-start.11
  166.5 1.5 copy-start.12
  172.7 0.7 copy-start.23
  457.9 1.9 copy-start.22
Sparse Core Ops, SparseCore 0:
  172.9 277.0 all-reduce.1
where the time goes:
time: 483 us; the launch traced here: 475 us
  waiting for transfers between devices  320 us (66%)
  local copies, waits for them, and re-layouts  45.4 us (9%)
  other arithmetic  35.1 us (7%)
  between operations  27.2 us (6%)
  matrix products  24.7 us (5%)
  loops' own time  14.1 us (3%)
  starting transfers between devices  8.56 us (2%)
    psum x1, waiting for transfers between devices, local(): summed_all = lax.psum(partial_value, ('gx', 'gy'))  276 us
    ppermute x2, waiting for transfers between devices, with_halo(): lax.ppermute(lax.slice_in_dim(block, block.shape[dim] - width, None, axis...  36.4 us
    unnamed x53, local copies, waits for them, and re-layouts  14.2 us
    concatenate x1, other arithmetic, with_halo(): block = jnp.concatenate([low, block, high], axis=dim)  10.9 us
    another operation x4, loops' own time, make_source(): lax.cond(heading < 2, lambda: eigen_vecs, lambda: colour_apply(chosen_lin...  10.1 us
  transfers between devices with their start and end apart: 5, of which 5 were waited for; matrix products, arithmetic and copies ran while one was open for 0% of the time, Pallas kernels for 0%

commit v1 on v0

v1 whole, which is shorter than its diff:
```python
import math

import jax
import jax.numpy as jnp
from jax import lax
from jax.experimental import pallas as pl
from jax.experimental.pallas import tpu as pltpu
from jax.sharding import PartitionSpec as P

MESH = pl.DeviceIdType.MESH
F32 = jnp.float32
BF16 = jnp.bfloat16
NX_RING, NY_RING, NZ_RING, CORES = 4, 4, 8, 2
LANES = 128


def device_at(core, x, y, z):
    return (((y % 2) * NZ_RING + z) * CORES + core, x * 2 + y // 2)


def reduce_kernel(norm, ev, links, out, vt, right, face_f, face, halo_y, halo_yf, halo_x, send0, own, recv0,
                  send1, recv1, own2, send2, recv2, own3, send3, recv3,
                  halo_send, halo_recv, core_send, core_recv, ring_send, ring_recv, z_send, z_recv):
    gx, gy = lax.axis_index("gx"), lax.axis_index("gy")
    core, z = gx % 2, (gx // 2) % NZ_RING
    x, y = gy // 2, (gy % 2) * 2 + gx // (2 * NZ_RING)
    n_gx, n_gy = 2 * 2 * NZ_RING, 2 * NX_RING
    sibling = device_at(1 - core, x, y, z)

    def at_x(d):
        return device_at(core, (x + d) % NX_RING, y, z)

    def at_y(d):
        return device_at(core, x, (y + d) % NY_RING, z)

    def at_z(d):
        return device_at(core, x, y, (z + d) % NZ_RING)

    before_x, after_x = ((gx + n_gx - 1) % n_gx, gy), ((gx + 1) % n_gx, gy)
    before_y, after_y = (gx, (gy + n_gy - 1) % n_gy), (gx, (gy + 1) % n_gy)

    barrier = pltpu.get_barrier_semaphore()
    peers = [before_x, after_x, before_y, after_y, sibling]
    peers += [at_x(d) for d in range(1, NX_RING)]
    peers += [at_y(d) for d in range(1, NY_RING)]
    peers += [at_z(d) for d in range(1, NZ_RING)]
    for peer in peers:
        pl.semaphore_signal(barrier, inc=1, device_id=peer, device_id_type=MESH)

    planes = ev.shape[2]

    def take_face(s, carry):
        for p in range(2):
            for c in range(3):
                face_f[pl.ds((p * 3 + c) * planes + s, 1), :] = ev[p, c, s].astype(F32)[0:1, :]
        return carry

    lax.fori_loop(0, planes, take_face, 0)
    face[...] = face_f[...].astype(BF16)
    pl.semaphore_wait(barrier, len(peers))

    started = []

    def send(src, dst, s_sem, r_sem, to):
        copy = pltpu.make_async_remote_copy(
            src_ref=src, dst_ref=dst, send_sem=s_sem, recv_sem=r_sem, device_id=to, device_id_type=MESH
        )
        copy.start()
        started.append(copy)
        return copy

    copy_y = send(face, halo_y, halo_send.at[0], halo_recv.at[0], before_y)
    nz = planes // 4
    copies_x = []
    for zz in range(nz):
        copies_x.append(
            send(ev.at[:, :, zz * 4], halo_x.at[:, :, zz], halo_send.at[1 + zz], halo_recv.at[1 + zz], before_x)
        )

    vt[...] = ev[...].reshape(-1, ev.shape[-1]).T

    def colour(h, s, source):
        cols = links[pl.ds((1 - h) * 18 * planes + s, 18, stride=planes), :].T
        coef = [jnp.broadcast_to(cols[:, i : i + 1], (16, LANES)) for i in range(18)]
        for lane in range(ev.shape[-1] // LANES):
            at = slice(lane * LANES, (lane + 1) * LANES)
            v = [[source(p, c, at) for c in range(3)] for p in range(2)]
            for a in range(3):
                re = im = None
                for b in range(3):
                    u_re, u_im = coef[a * 3 + b], coef[9 + a * 3 + b]
                    t_re = u_re * v[0][b] - u_im * v[1][b]
                    t_im = u_re * v[1][b] + u_im * v[0][b]
                    re = t_re if re is None else re + t_re
                    im = t_im if im is None else im + t_im
                re, im = re.astype(BF16), im.astype(BF16)
                right[h, 0, 0, a, s, :, at] = re
                right[h, 0, 1, a, s, :, at] = im
                right[h, 1, 0, a, s, :, at] = im
                right[h, 1, 1, a, s, :, at] = -re

    def gram(h, q):
        lhs = vt[...]
        wide = 2 * LANES
        for j in range(ev.shape[-1] // wide):
            rhs = right[h, q, :, :, :, :, j * wide : (j + 1) * wide].reshape(-1, wide)
            yield j, jnp.dot(lhs, rhs, preferred_element_type=F32) * norm

    rows = ev.shape[-1]

    def gram_other(h):
        for j, value in gram(h, 1 - core):
            for half in range(2):
                send0[h, (2 * j + half) * rows : (2 * j + half + 1) * rows, :] = value[
                    :, half * LANES : (half + 1) * LANES
                ].astype(BF16)
        return send(send0.at[h], recv0.at[h], core_send.at[h, 0], core_recv.at[h, 0], sibling)

    def gram_own(h):
        for j, value in gram(h, core):
            for half in range(2):
                own[h, (2 * j + half) * rows : (2 * j + half + 1) * rows, :] = value[
                    :, half * LANES : (half + 1) * LANES
                ]

    first = ((x, at_x), (y, at_y))
    second = ((y, at_y), (x, at_x))
    len1, len2, len3 = own.shape[1] // 4, own.shape[1] // 16, own.shape[1] // 128

    def start1(h, copy):
        copy.wait_recv()
        total = own[h] + recv0[h].astype(F32)
        own[h] = total
        send1[h] = total.astype(BF16)
        place, at = first[h]
        return [
            send(send1.at[h, pl.ds((place + d) % 4 * len1, len1)], recv1.at[h, d - 1],
                 ring_send.at[h, 0, d - 1], ring_recv.at[h, 0, d - 1], at(d))
            for d in range(1, 4)
        ]

    def start2(h, copies):
        total = own[h, pl.ds(first[h][0] * len1, len1)]
        for d, copy in enumerate(copies):
            copy.wait_recv()
            total = total + recv1[h, d].astype(F32)
        own2[h] = total
        send2[h] = total.astype(BF16)
        place, at = second[h]
        return [
            send(send2.at[h, pl.ds((place + d) % 4 * len2, len2)], recv2.at[h, d - 1],
                 ring_send.at[h, 1, d - 1], ring_recv.at[h, 1, d - 1], at(d))
            for d in range(1, 4)
        ]

    def start3(h, copies):
        total = own2[h, pl.ds(second[h][0] * len2, len2)]
        for d, copy in enumerate(copies):
            copy.wait_recv()
            total = total + recv2[h, d].astype(F32)
        own3[h] = total
        send3[h] = total.astype(BF16)
        return [
            send(send3.at[h, pl.ds((z + d) % NZ_RING * len3, len3)], recv3.at[h, d - 1],
                 z_send.at[h, 0, d - 1], z_recv.at[h, 0, d - 1], at_z(d))
            for d in range(1, NZ_RING)
        ]

    def base(h):
        b0 = core * own.shape[1]
        b1 = b0 + first[h][0] * len1
        b2 = b1 + second[h][0] * len2
        return b0, b1, b2, b2 + z * len3

    def gather3(h, copies):
        total = own3[h, pl.ds(z * len3, len3)]
        for d, copy in enumerate(copies):
            copy.wait_recv()
            total = total + recv3[h, d].astype(F32)
        place = pl.ds(base(h)[3], len3)
        out[h, place] = total.astype(BF16)
        return [
            send(out.at[h, place], out.at[h, place], z_send.at[h, 1, d - 1], z_recv.at[h, 1, d - 1], at_z(d))
            for d in range(1, NZ_RING)
        ]

    def gather2(h, copies):
        for copy in copies:
            copy.wait_recv()
        place = pl.ds(base(h)[2], len2)
        at = second[h][1]
        return [
            send(out.at[h, place], out.at[h, place], ring_send.at[h, 2, d - 1], ring_recv.at[h, 2, d - 1], at(d))
            for d in range(1, 4)
        ]

    def to_sibling(h, d, place):
        return send(out.at[h, place], out.at[h, place], core_send.at[h, 1 + d], core_recv.at[h, 1 + d], sibling)

    def gather1(h, copies):
        for copy in copies:
            copy.wait_recv()
        place = pl.ds(base(h)[1], len1)
        at = first[h][1]
        ring = [
            send(out.at[h, place], out.at[h, place], ring_send.at[h, 3, d - 1], ring_recv.at[h, 3, d - 1], at(d))
            for d in range(1, 4)
        ]
        return ring, [to_sibling(h, 0, place)]

    def gather0(h, both):
        ring, across = both
        for d in (1, 3, 2):
            ring[d - 1].wait_recv()
            place = pl.ds(base(h)[0] + (first[h][0] + 4 - d) % 4 * len1, len1)
            across.append(to_sibling(h, d, place))
        return across

    def hop_x_inner(zz, carry):
        for xx in range(3):
            s = zz * 4 + xx
            colour(1, s, lambda p, c, at: ev[p, c, s + 1, :, at].astype(F32))
        return carry

    def hop_x_last(zz, carry):
        colour(1, zz * 4 + 3, lambda p, c, at: halo_x[p, c, zz, :, at].astype(F32))
        return carry

    def hop_y(s, carry):
        last = lax.broadcasted_iota(jnp.int32, (16, LANES), 0) == 15
        edges = [halo_yf[j, pl.ds(s, 6, stride=planes), :] for j in range(halo_yf.shape[0])]

        def source(p, c, at):
            value = pltpu.roll(ev[p, c, s, :, at].astype(F32), 15, 0)
            edge = edges[at.start // LANES][p * 3 + c : p * 3 + c + 1, :]
            return jnp.where(last, jnp.broadcast_to(edge, value.shape), value)

        colour(0, s, source)
        return carry

    lax.fori_loop(0, nz, hop_x_inner, 0)
    copy_y.wait_recv()
    for j in range(halo_yf.shape[0]):
        halo_yf[j] = halo_y[:, j * LANES : (j + 1) * LANES].astype(F32)
    lax.fori_loop(0, planes, hop_y, 0)
    a = gram_other(0)
    gram_own(0)
    a = start1(0, a)
    for copy in copies_x:
        copy.wait_recv()
    lax.fori_loop(0, nz, hop_x_last, 0)
    b = gram_other(1)
    a = start2(0, a)
    gram_own(1)
    b = start1(1, b)
    a = start3(0, a)
    a = gather3(0, a)
    b = start2(1, b)
    a = gather2(0, a)
    b = start3(1, b)
    a = gather1(0, a)
    b = gather3(1, b)
    a = gather0(0, a)
    b = gather2(1, b)
    b = gather1(1, b)
    b = gather0(1, b)
    for copy in a + b:
        copy.wait_recv()
    for copy in started:
        copy.wait_send()


def contract_kernel(directions, spins, g, peram, elementals, contracted, products):
    gx = lax.axis_index("gx")
    vecs = peram.shape[-1] // 4
    rows = peram.shape[1]
    own_rows = elementals.shape[2]
    pieces = [peram[p].astype(F32)[:, t * vecs : (t + 1) * vecs] for p in range(2) for t in range(4)]
    pick = lax.broadcasted_iota(jnp.int32, (own_rows, vecs), 1) == gx * own_rows + lax.broadcasted_iota(
        jnp.int32, (own_rows, vecs), 0
    )
    lhs = jnp.concatenate(pieces + [jnp.where(pick, 1.0, 0.0)], axis=0).astype(BF16)
    m = 4 * rows
    for h in range(2):
        parts = []
        for q in range(2):
            blocks = [g[h, (q * 4 + j) * vecs : (q * 4 + j + 1) * vecs, :] for j in range(4)]
            parts.append(jnp.concatenate(blocks, axis=1))
        re = jnp.dot(lhs, parts[0], preferred_element_type=F32)
        im = jnp.dot(lhs, parts[1], preferred_element_type=F32)
        products[h, 0] = jnp.concatenate([re[:m] - im[m : 2 * m], re[2 * m :]], 0)
        products[h, 1] = jnp.concatenate([im[:m] + re[m : 2 * m], im[2 * m :]], 0)
        over = (((1,), (1,)), ((), ()))
        re = lax.dot_general(lhs, parts[0], over, preferred_element_type=F32)
        im = lax.dot_general(lhs, parts[1], over, preferred_element_type=F32)
        products[2 + h, 0] = jnp.concatenate([re[:m] + im[m : 2 * m], re[2 * m :]], 0)
        products[2 + h, 1] = jnp.concatenate([re[m : 2 * m] - im[:m], -im[2 * m :]], 0)
    for k in range(4):
        which = jnp.where(directions[k] % 2 == 0, directions[k] + 1, directions[k] - 1)
        for q in range(2):
            elementals[k, q] = products[which, q, m : m + own_rows, :]
            for u in range(4):
                row = pl.multiple_of(spins[u] * rows, rows)
                contracted[k, q, :, u * vecs : (u + 1) * vecs] = products[which, q, pl.ds(row, rows), :].astype(BF16)


def local(eigen_vecs, gauge_links, directions, spin_map, perambulator):
    reim, colours, nz, nx, ny, vecs = eigen_vecs.shape
    sites = nz * nx * ny * lax.axis_size("gx") * lax.axis_size("gy")
    norm = 1.0 / math.sqrt(3.0 * sites)
    planes = nz * nx
    ev = eigen_vecs.reshape(reim, colours, planes, ny, vecs)
    links = gauge_links.reshape(-1, ny)
    half = vecs * vecs // LANES
    vmem = pl.BlockSpec(memory_space=pltpu.VMEM)
    faces = reim * colours * planes
    g = pl.pallas_call(
        lambda *refs: reduce_kernel(norm, *refs),
        out_shape=jax.ShapeDtypeStruct((2, 2 * half, LANES), BF16),
        in_specs=[vmem, vmem],
        out_specs=vmem,
        scratch_shapes=[
            pltpu.VMEM((vecs, reim * colours * planes * ny), BF16),
            pltpu.VMEM((2, 2, reim, colours, planes, ny, vecs), BF16),
            pltpu.VMEM((faces, vecs), F32),
            pltpu.VMEM((faces, vecs), BF16),
            pltpu.VMEM((faces, vecs), BF16),
            pltpu.VMEM((vecs // LANES, faces, LANES), F32),
            pltpu.VMEM((reim, colours, nz, ny, vecs), BF16),
            pltpu.VMEM((2, half, LANES), BF16),
            pltpu.VMEM((2, half, LANES), F32),
            pltpu.VMEM((2, half, LANES), BF16),
            pltpu.VMEM((2, half, LANES), BF16),
            pltpu.VMEM((2, 3, half // 4, LANES), BF16),
            pltpu.VMEM((2, half // 4, LANES), F32),
            pltpu.VMEM((2, half // 4, LANES), BF16),
            pltpu.VMEM((2, 3, half // 16, LANES), BF16),
            pltpu.VMEM((2, half // 16, LANES), F32),
            pltpu.VMEM((2, half // 16, LANES), BF16),
            pltpu.VMEM((2, NZ_RING - 1, half // 128, LANES), BF16),
            pltpu.SemaphoreType.DMA((1 + nz,)),
            pltpu.SemaphoreType.DMA((1 + nz,)),
            pltpu.SemaphoreType.DMA((2, 5)),
            pltpu.SemaphoreType.DMA((2, 5)),
            pltpu.SemaphoreType.DMA((2, 4, 3)),
            pltpu.SemaphoreType.DMA((2, 4, 3)),
            pltpu.SemaphoreType.DMA((2, 2, NZ_RING - 1)),
            pltpu.SemaphoreType.DMA((2, 2, NZ_RING - 1)),
        ],
        compiler_params=pltpu.CompilerParams(
            collective_id=0, has_side_effects=True, vmem_limit_bytes=48 * 2**20
        ),
        name="reduce",
    )(ev, links)
    rows = perambulator.shape[1]
    own_rows = vecs // lax.axis_size("gx")
    smem = pl.BlockSpec(memory_space=pltpu.SMEM)
    return pl.pallas_call(
        contract_kernel,
        out_shape=(
            jax.ShapeDtypeStruct((4, 2, own_rows, vecs), F32),
            jax.ShapeDtypeStruct((4, 2, rows, 4 * vecs), BF16),
        ),
        in_specs=[smem, smem, vmem, vmem],
        out_specs=(vmem, vmem),
        scratch_shapes=[pltpu.VMEM((4, 2, 4 * rows + own_rows, vecs), F32)],
        compiler_params=pltpu.CompilerParams(vmem_limit_bytes=32 * 2**20),
        name="contract",
    )(directions, spin_map, g, perambulator)


def solution(mesh):
    in_specs = (
        P(None, None, None, "gx", "gy", None),
        P(None, None, None, None, None, "gx", "gy"),
        P(),
        P(),
        P(None, ("gx", "gy"), None),
    )
    out_specs = (P(None, None, "gx", None), P(None, None, ("gx", "gy"), None))
    return jax.shard_map(local, mesh=mesh, in_specs=in_specs, out_specs=out_specs, check_vma=False)
```

time: 483 us -> 76.4 us (0.16); the launches traced: 475 us -> 76.3 us
  waiting for transfers between devices: 320 us -> 0 us
  Pallas kernels: 0 us -> 73.2 us
  local copies, waits for them, and re-layouts: 45.4 us -> 2.39 us
  other arithmetic: 35.1 us -> 0 us
  between operations: 27.2 us -> 0.69 us
  matrix products: 24.7 us -> 0 us
  loops' own time: 14.1 us -> 0 us
  starting transfers between devices: 8.56 us -> 0 us
    psum x1 -> x0, waiting for transfers between devices: 276 us -> none  [local(): summed_all = lax.psum(partial_value, ('gx', 'gy'))]
    pallas_call x0 -> x2, Pallas kernels: none -> 73.2 us  [the longest x1 70.7 us: local(): pl.pallas_call(lambda *refs: reduce_kernel(norm, *refs), out_shape=jax.Sh...]
    ppermute x4 -> x0, waiting for transfers between devices: 44.1 us -> none  [the longest x2 36.4 us: with_halo(): lax.ppermute(lax.slice_in_dim(block, block.shape[dim] - width, None, axis...]
    dot_general x21 -> x0, matrix products: 24.7 us -> none  [the longest x4 5.99 us: gram_term(): jnp.dot(left_im.T, right_im, preferred_element_type=jnp.float32)]
    another operation x8 -> x0, loops' own time: 14.1 us -> none  [the longest x4 10.1 us: make_source(): lax.cond(heading < 2, lambda: eigen_vecs, lambda: colour_apply(chosen_lin...]
    unnamed x53 -> x10, local copies, waits for them, and re-layouts: 14.2 us -> 2.39 us
    concatenate x1 -> x0, other arithmetic: 10.9 us -> none  [with_halo(): block = jnp.concatenate([low, block, high], axis=dim)]
    another operation x20 -> x0, other arithmetic: 9.24 us -> none
  transfers between devices with their start and end apart: 5 -> 0, of which waited for: 5 -> 0; matrix products, arithmetic and copies ran while one was open for 0% -> 0% of each run, Pallas kernels for 0% -> 0%
where the time goes in v1:
time: 76.4 us; the launch traced here: 76.3 us
  Pallas kernels  73.2 us (96%)
  local copies, waits for them, and re-layouts  2.39 us (3%)
    pallas_call x1, Pallas kernels, local(): pl.pallas_call(lambda *refs: reduce_kernel(norm, *refs), out_shape=jax.Sh...  70.7 us
    pallas_call x1, Pallas kernels, local(): pl.pallas_call(contract_kernel, out_shape=(jax.ShapeDtypeStruct((4, 2, ow...  2.47 us
    unnamed x10, local copies, waits for them, and re-layouts  2.39 us

profile of v1, /device:TPU:1, one launch (start us, length us, event | category | flops | bytes accessed | tf_op | source)
XLA Modules:
  0.0 76.3 jit_solution(5982458175030877220)
XLA Ops:
  0.6 0.0 copy-start.4
  0.6 0.0 copy-start.3
  0.7 0.0 copy-start
  0.7 1.4 %copy-done = bf16[2,3,4,4,16,512]{5,4,3,2,1,0:T(8,128)(2,1)S(1)} copy-done((bf16[2,3,4,4,16,512]{5,4,3,2,1,0:T(8,128)(2,1)S(1)}, bf16[2,3,4,4,16,512]{5,4,3,2,1,0:T(8,128)(2,1)}, u32[]{:S(2)}) %copy-start) | copy-done | bytes 1572888
  2.1 0.0 copy-start.1
  2.1 1.0 %copy-done.1 = f32[2,2,3,3,4,4,16]{6,5,4,3,2,1,0:T(4,128)S(1)} copy-done((f32[2,2,3,3,4,4,16]{6,5,4,3,2,1,0:T(4,128)S(1)}, f32[2,2,3,3,4,4,16]{6,5,4,3,2,1,0:T(4,128)}, u32[]{:S(2)}) %copy-start.1) | copy-done | bytes 36888
  3.0 0.0 copy-start.2
  3.0 70.7 %reduce.1.g = bf16[2,4096,128]{2,1,0:T(8,128)(2,1)S(1)} custom-call(bf16[2,3,16,16,512]{4,3,2,1,0:T(8,128)(2,1)S(1)} %bitcast.2, f32[576,16]{1,0:T(8,128)S(1)} %bitcast.3), custom_call_target="tpu_custom_call" | custom-call | tf_op jit(solution)/shard_map/reduce/pallas_call | solution.py:317
  73.8 0.0 copy-done.4
  73.8 0.0 copy-done.3
  73.8 0.0 copy-done.2
  73.8 2.5 %contract.1 = (f32[4,2,16,512]{3,2,1,0:T(8,128)}, bf16[4,2,8,2048]{3,2,1,0:T(8,128)(2,1)}) custom-call(s32[4]{0:T(128)S(1)} %copy-done.3, s32[4]{0:T(128)S(1)} %copy-done.4, bf16[2,4096,128]{2,1,0:T(8,128)(2,1)S(1)} %reduce.1.g, bf16[2,8,2048]{2,1,0:T(8,128)(2,1)S(1)} %copy-done.2), custom_call_target="tpu_custom_call" | custom-call | tf_op jit(solution)/shard_map/contract/pallas_call | solution.py:358
Async XLA Ops:
  0.6 73.2 %copy-start.4 = (s32[4]{0:T(128)S(1)}, s32[4]{0:T(128)}, u32[]{:S(2)}) copy-start(s32[4]{0:T(128)} %spins.1) | copy-start | bytes 52
  0.6 73.2 %copy-start.3 = (s32[4]{0:T(128)S(1)}, s32[4]{0:T(128)}, u32[]{:S(2)}) copy-start(s32[4]{0:T(128)} %directions.1) | copy-start | bytes 52
  0.7 1.4 %copy-start = (bf16[2,3,4,4,16,512]{5,4,3,2,1,0:T(8,128)(2,1)S(1)}, bf16[2,3,4,4,16,512]{5,4,3,2,1,0:T(8,128)(2,1)}, u32[]{:S(2)}) copy-start(bf16[2,3,4,4,16,512]{5,4,3,2,1,0:T(8,128)(2,1)} %param.5) | copy-start | bytes 4718596
  2.1 1.0 %copy-start.1 = (f32[2,2,3,3,4,4,16]{6,5,4,3,2,1,0:T(4,128)S(1)}, f32[2,2,3,3,4,4,16]{6,5,4,3,2,1,0:T(4,128)}, u32[]{:S(2)}) copy-start(f32[2,2,3,3,4,4,16]{6,5,4,3,2,1,0:T(4,128)} %param.6) | copy-start | bytes 110596
  3.0 70.8 %copy-start.2 = (bf16[2,8,2048]{2,1,0:T(8,128)(2,1)S(1)}, bf16[2,8,2048]{2,1,0:T(8,128)(2,1)}, u32[]{:S(2)}) copy-start(bf16[2,8,2048]{2,1,0:T(8,128)(2,1)} %peram.1) | copy-start | bytes 196612

commit v2 on v1

--- a/solution.py
+++ b/solution.py
@@ -18,9 +18,9 @@
     return (((y % 2) * NZ_RING + z) * CORES + core, x * 2 + y // 2)
 
 
-def reduce_kernel(norm, ev, links, out, vt, right, face_f, face, halo_y, halo_yf, halo_x, send0, own, recv0,
-                  send1, recv1, own2, send2, recv2, own3, send3, recv3,
-                  halo_send, halo_recv, core_send, core_recv, ring_send, ring_recv, z_send, z_recv):
+def reduce_kernel(norm, ev_in, links_in, out, ev, links, vt, right, face_f, face, halo_y, halo_yf, halo_x, send0, own, recv0,
+                  send1, recv1, own2, send2, recv2, own3, send3, recv3, done3,
+                  load, halo_send, halo_recv, core_send, core_recv, ring_send, ring_recv, z_send, z_recv):
     gx, gy = lax.axis_index("gx"), lax.axis_index("gy")
     core, z = gx % 2, (gx // 2) % NZ_RING
     x, y = gy // 2, (gy % 2) * 2 + gx // (2 * NZ_RING)
@@ -39,6 +39,9 @@
     before_x, after_x = ((gx + n_gx - 1) % n_gx, gy), ((gx + 1) % n_gx, gy)
     before_y, after_y = (gx, (gy + n_gy - 1) % n_gy), (gx, (gy + 1) % n_gy)
 
+    loads = [pltpu.make_async_copy(ev_in, ev, load.at[0]), pltpu.make_async_copy(links_in, links, load.at[1])]
+    for copy in loads:
+        copy.start()
     barrier = pltpu.get_barrier_semaphore()
     peers = [before_x, after_x, before_y, after_y, sibling]
     peers += [at_x(d) for d in range(1, NX_RING)]
@@ -55,6 +58,7 @@
                 face_f[pl.ds((p * 3 + c) * planes + s, 1), :] = ev[p, c, s].astype(F32)[0:1, :]
         return carry
 
+    loads[0].wait()
     lax.fori_loop(0, planes, take_face, 0)
     face[...] = face_f[...].astype(BF16)
     pl.semaphore_wait(barrier, len(peers))
@@ -74,7 +78,7 @@
     copies_x = []
     for zz in range(nz):
         copies_x.append(
-            send(ev.at[:, :, zz * 4], halo_x.at[:, :, zz], halo_send.at[1 + zz], halo_recv.at[1 + zz], before_x)
+            send(ev_in.at[:, :, zz * 4], halo_x.at[:, :, zz], halo_send.at[1 + zz], halo_recv.at[1 + zz], before_x)
         )
 
     vt[...] = ev[...].reshape(-1, ev.shape[-1]).T
@@ -125,95 +129,118 @@
 
     first = ((x, at_x), (y, at_y))
     second = ((y, at_y), (x, at_x))
-    len1, len2, len3 = own.shape[1] // 4, own.shape[1] // 16, own.shape[1] // 128
+    half = own.shape[1]
+    part, len1, len2, len3 = half // 2, half // 8, half // 32, half // 256
 
     def start1(h, copy):
         copy.wait_recv()
         total = own[h] + recv0[h].astype(F32)
         own[h] = total
         send1[h] = total.astype(BF16)
-        place, at = first[h]
         return [
-            send(send1.at[h, pl.ds((place + d) % 4 * len1, len1)], recv1.at[h, d - 1],
-                 ring_send.at[h, 0, d - 1], ring_recv.at[h, 0, d - 1], at(d))
-            for d in range(1, 4)
+            [
+                send(send1.at[h, pl.ds(s * part + (first[s][0] + d) % 4 * len1, len1)], recv1.at[h, s, d - 1],
+                     ring_send.at[h, 0, s, d - 1], ring_recv.at[h, 0, s, d - 1], first[s][1](d))
+                for d in range(1, 4)
+            ]
+            for s in range(2)
         ]
 
     def start2(h, copies):
-        total = own[h, pl.ds(first[h][0] * len1, len1)]
-        for d, copy in enumerate(copies):
-            copy.wait_recv()
-            total = total + recv1[h, d].astype(F32)
-        own2[h] = total
-        send2[h] = total.astype(BF16)
-        place, at = second[h]
-        return [
-            send(send2.at[h, pl.ds((place + d) % 4 * len2, len2)], recv2.at[h, d - 1],
-                 ring_send.at[h, 1, d - 1], ring_recv.at[h, 1, d - 1], at(d))
-            for d in range(1, 4)
-        ]
+        result = []
+        for s in range(2):
+            total = own[h, pl.ds(s * part + first[s][0] * len1, len1)]
+            for d, copy in enumerate(copies[s]):
+                copy.wait_recv()
+                total = total + recv1[h, s, d].astype(F32)
+            own2[h, s] = total
+            send2[h, s] = total.astype(BF16)
+            place, at = second[s]
+            result.append([
+                send(send2.at[h, s, pl.ds((place + d) % 4 * len2, len2)], recv2.at[h, s, d - 1],
+                     ring_send.at[h, 1, s, d - 1], ring_recv.at[h, 1, s, d - 1], at(d))
+                for d in range(1, 4)
+            ])
+        return result
 
     def start3(h, copies):
-        total = own2[h, pl.ds(second[h][0] * len2, len2)]
-        for d, copy in enumerate(copies):
-            copy.wait_recv()
-            total = total + recv2[h, d].astype(F32)
+        totals = []
+        for s in range(2):
+            total = own2[h, s, pl.ds(second[s][0] * len2, len2)]
+            for d, copy in enumerate(copies[s]):
+                copy.wait_recv()
+                total = total + recv2[h, s, d].astype(F32)
+            totals.append(total)
+        total = jnp.concatenate(
+            [totals[s][i * len3 : (i + 1) * len3] for i in range(NZ_RING) for s in range(2)], axis=0
+        )
         own3[h] = total
         send3[h] = total.astype(BF16)
         return [
-            send(send3.at[h, pl.ds((z + d) % NZ_RING * len3, len3)], recv3.at[h, d - 1],
+            send(send3.at[h, pl.ds((z + d) % NZ_RING * 2 * len3, 2 * len3)], recv3.at[h, d - 1],
                  z_send.at[h, 0, d - 1], z_recv.at[h, 0, d - 1], at_z(d))
             for d in range(1, NZ_RING)
         ]
 
-    def base(h):
-        b0 = core * own.shape[1]
-        b1 = b0 + first[h][0] * len1
-        b2 = b1 + second[h][0] * len2
-        return b0, b1, b2, b2 + z * len3
+    def base(s):
+        b0 = core * half + s * part
+        b1 = b0 + first[s][0] * len1
+        return b0, b1, b1 + second[s][0] * len2
 
     def gather3(h, copies):
-        total = own3[h, pl.ds(z * len3, len3)]
+        place = pl.ds(z * 2 * len3, 2 * len3)
+        total = own3[h, place]
         for d, copy in enumerate(copies):
             copy.wait_recv()
             total = total + recv3[h, d].astype(F32)
-        place = pl.ds(base(h)[3], len3)
-        out[h, place] = total.astype(BF16)
+        done3[h, place] = total.astype(BF16)
         return [
-            send(out.at[h, place], out.at[h, place], z_send.at[h, 1, d - 1], z_recv.at[h, 1, d - 1], at_z(d))
+            send(done3.at[h, place], done3.at[h, place], z_send.at[h, 1, d - 1], z_recv.at[h, 1, d - 1], at_z(d))
             for d in range(1, NZ_RING)
         ]
 
     def gather2(h, copies):
         for copy in copies:
             copy.wait_recv()
-        place = pl.ds(base(h)[2], len2)
-        at = second[h][1]
-        return [
-            send(out.at[h, place], out.at[h, place], ring_send.at[h, 2, d - 1], ring_recv.at[h, 2, d - 1], at(d))
-            for d in range(1, 4)
-        ]
-
-    def to_sibling(h, d, place):
-        return send(out.at[h, place], out.at[h, place], core_send.at[h, 1 + d], core_recv.at[h, 1 + d], sibling)
+        value = done3[h].astype(F32)
+        result = []
+        for s in range(2):
+            place = pl.ds(base(s)[2], len2)
+            out[h, place] = jnp.concatenate(
+                [value[(2 * i + s) * len3 : (2 * i + s + 1) * len3] for i in range(NZ_RING)], axis=0
+            ).astype(BF16)
+            result += [
+                send(out.at[h, place], out.at[h, place], ring_send.at[h, 2, s, d - 1], ring_recv.at[h, 2, s, d - 1],
+                     second[s][1](d))
+                for d in range(1, 4)
+            ]
+        return result
+
+    def to_sibling(h, s, d, place):
+        return send(out.at[h, place], out.at[h, place], core_send.at[h, 1 + 4 * s + d], core_recv.at[h, 1 + 4 * s + d],
+                    sibling)
 
     def gather1(h, copies):
         for copy in copies:
             copy.wait_recv()
-        place = pl.ds(base(h)[1], len1)
-        at = first[h][1]
-        ring = [
-            send(out.at[h, place], out.at[h, place], ring_send.at[h, 3, d - 1], ring_recv.at[h, 3, d - 1], at(d))
-            for d in range(1, 4)
-        ]
-        return ring, [to_sibling(h, 0, place)]
+        rings, across = [], []
+        for s in range(2):
+            place = pl.ds(base(s)[1], len1)
+            rings.append([
+                send(out.at[h, place], out.at[h, place], ring_send.at[h, 3, s, d - 1], ring_recv.at[h, 3, s, d - 1],
+                     first[s][1](d))
+                for d in range(1, 4)
+            ])
+            across.append(to_sibling(h, s, 0, place))
+        return rings, across
 
     def gather0(h, both):
-        ring, across = both
+        rings, across = both
         for d in (1, 3, 2):
-            ring[d - 1].wait_recv()
-            place = pl.ds(base(h)[0] + (first[h][0] + 4 - d) % 4 * len1, len1)
-            across.append(to_sibling(h, d, place))
+            for s in range(2):
+                rings[s][d - 1].wait_recv()
+                place = pl.ds(base(s)[0] + (first[s][0] + 4 - d) % 4 * len1, len1)
+                across.append(to_sibling(h, s, d, place))
         return across
 
     def hop_x_inner(zz, carry):
@@ -238,6 +265,7 @@
         colour(0, s, source)
         return carry
 
+    loads[1].wait()
     lax.fori_loop(0, nz, hop_x_inner, 0)
     copy_y.wait_recv()
     for j in range(halo_yf.shape[0]):
@@ -250,20 +278,11 @@
         copy.wait_recv()
     lax.fori_loop(0, nz, hop_x_last, 0)
     b = gram_other(1)
-    a = start2(0, a)
     gram_own(1)
     b = start1(1, b)
-    a = start3(0, a)
-    a = gather3(0, a)
-    b = start2(1, b)
-    a = gather2(0, a)
-    b = start3(1, b)
-    a = gather1(0, a)
-    b = gather3(1, b)
-    a = gather0(0, a)
-    b = gather2(1, b)
-    b = gather1(1, b)
-    b = gather0(1, b)
+    for step in (start2, start3, gather3, gather2, gather1, gather0):
+        a = step(0, a)
+        b = step(1, b)
     for copy in a + b:
         copy.wait_recv()
     for copy in started:
@@ -317,9 +336,11 @@
     g = pl.pallas_call(
         lambda *refs: reduce_kernel(norm, *refs),
         out_shape=jax.ShapeDtypeStruct((2, 2 * half, LANES), BF16),
-        in_specs=[vmem, vmem],
+        in_specs=[pl.BlockSpec(memory_space=pltpu.HBM)] * 2,
         out_specs=vmem,
         scratch_shapes=[
+            pltpu.VMEM(ev.shape, BF16),
+            pltpu.VMEM(links.shape, F32),
             pltpu.VMEM((vecs, reim * colours * planes * ny), BF16),
             pltpu.VMEM((2, 2, reim, colours, planes, ny, vecs), BF16),
             pltpu.VMEM((faces, vecs), F32),
@@ -331,19 +352,21 @@
             pltpu.VMEM((2, half, LANES), F32),
             pltpu.VMEM((2, half, LANES), BF16),
             pltpu.VMEM((2, half, LANES), BF16),
-            pltpu.VMEM((2, 3, half // 4, LANES), BF16),
-            pltpu.VMEM((2, half // 4, LANES), F32),
-            pltpu.VMEM((2, half // 4, LANES), BF16),
-            pltpu.VMEM((2, 3, half // 16, LANES), BF16),
+            pltpu.VMEM((2, 2, 3, half // 8, LANES), BF16),
+            pltpu.VMEM((2, 2, half // 8, LANES), F32),
+            pltpu.VMEM((2, 2, half // 8, LANES), BF16),
+            pltpu.VMEM((2, 2, 3, half // 32, LANES), BF16),
             pltpu.VMEM((2, half // 16, LANES), F32),
             pltpu.VMEM((2, half // 16, LANES), BF16),
             pltpu.VMEM((2, NZ_RING - 1, half // 128, LANES), BF16),
+            pltpu.VMEM((2, half // 16, LANES), BF16),
+            pltpu.SemaphoreType.DMA((2,)),
             pltpu.SemaphoreType.DMA((1 + nz,)),
             pltpu.SemaphoreType.DMA((1 + nz,)),
-            pltpu.SemaphoreType.DMA((2, 5)),
-            pltpu.SemaphoreType.DMA((2, 5)),
-            pltpu.SemaphoreType.DMA((2, 4, 3)),
-            pltpu.SemaphoreType.DMA((2, 4, 3)),
+            pltpu.SemaphoreType.DMA((2, 9)),
+            pltpu.SemaphoreType.DMA((2, 9)),
+            pltpu.SemaphoreType.DMA((2, 4, 2, 3)),
+            pltpu.SemaphoreType.DMA((2, 4, 2, 3)),
             pltpu.SemaphoreType.DMA((2, 2, NZ_RING - 1)),
             pltpu.SemaphoreType.DMA((2, 2, NZ_RING - 1)),
         ],

time: 76.4 us -> 63.7 us (0.83)
  Pallas kernels: 73.2 us -> 60.5 us
    pallas_call x1, Pallas kernels: 70.7 us -> 58 us  [local(): pl.pallas_call(lambda *refs: reduce_kernel(norm, *refs), out_shape=jax.Sh...]
where the time goes in v2:
time: 63.7 us; the launch traced here: 63.6 us
  Pallas kernels  60.5 us (95%)
  local copies, waits for them, and re-layouts  2.39 us (4%)
  between operations  0.69 us (1%)
    pallas_call x1, Pallas kernels, local(): pl.pallas_call(lambda *refs: reduce_kernel(norm, *refs), out_shape=jax.Sh...  58 us
    pallas_call x1, Pallas kernels, local(): pl.pallas_call(contract_kernel, out_shape=(jax.ShapeDtypeStruct((4, 2, ow...  2.47 us
    unnamed x10, local copies, waits for them, and re-layouts  2.39 us

profile of v2, /device:TPU:1, one launch (start us, length us, event | category | flops | bytes accessed | tf_op | source)
XLA Modules:
  0.0 63.6 jit_solution(15264390935499788310)
XLA Ops:
  0.6 0.0 copy-start.4
  0.6 0.0 copy-start.3
  0.7 0.0 copy-start
  0.7 1.4 %copy-done = bf16[2,3,4,4,16,512]{5,4,3,2,1,0:T(8,128)(2,1)S(1)} copy-done((bf16[2,3,4,4,16,512]{5,4,3,2,1,0:T(8,128)(2,1)S(1)}, bf16[2,3,4,4,16,512]{5,4,3,2,1,0:T(8,128)(2,1)}, u32[]{:S(2)}) %copy-start) | copy-done | bytes 1572888
  2.1 0.0 copy-start.1
  2.1 1.0 %copy-done.1 = f32[2,2,3,3,4,4,16]{6,5,4,3,2,1,0:T(4,128)S(1)} copy-done((f32[2,2,3,3,4,4,16]{6,5,4,3,2,1,0:T(4,128)S(1)}, f32[2,2,3,3,4,4,16]{6,5,4,3,2,1,0:T(4,128)}, u32[]{:S(2)}) %copy-start.1) | copy-done | bytes 36888
  3.0 0.0 copy-start.2
  3.0 58.0 %reduce.1.g = bf16[2,4096,128]{2,1,0:T(8,128)(2,1)S(1)} custom-call(bf16[2,3,16,16,512]{4,3,2,1,0:T(8,128)(2,1)S(1)} %bitcast.2, f32[576,16]{1,0:T(8,128)S(1)} %bitcast.3), custom_call_target="tpu_custom_call" | custom-call | tf_op jit(solution)/shard_map/reduce/pallas_call | solution.py:336
  61.1 0.0 copy-done.4
  61.1 0.0 copy-done.3
  61.1 0.0 copy-done.2
  61.1 2.5 %contract.1 = (f32[4,2,16,512]{3,2,1,0:T(8,128)}, bf16[4,2,8,2048]{3,2,1,0:T(8,128)(2,1)}) custom-call(s32[4]{0:T(128)S(1)} %copy-done.3, s32[4]{0:T(128)S(1)} %copy-done.4, bf16[2,4096,128]{2,1,0:T(8,128)(2,1)S(1)} %reduce.1.g, bf16[2,8,2048]{2,1,0:T(8,128)(2,1)S(1)} %copy-done.2), custom_call_target="tpu_custom_call" | custom-call | tf_op jit(solution)/shard_map/contract/pallas_call | solution.py:381
Async XLA Ops:
  0.6 60.4 %copy-start.4 = (s32[4]{0:T(128)S(1)}, s32[4]{0:T(128)}, u32[]{:S(2)}) copy-start(s32[4]{0:T(128)} %spins.1) | copy-start | bytes 52
  0.6 60.4 %copy-start.3 = (s32[4]{0:T(128)S(1)}, s32[4]{0:T(128)}, u32[]{:S(2)}) copy-start(s32[4]{0:T(128)} %directions.1) | copy-start | bytes 52
  0.7 1.4 %copy-start = (bf16[2,3,4,4,16,512]{5,4,3,2,1,0:T(8,128)(2,1)S(1)}, bf16[2,3,4,4,16,512]{5,4,3,2,1,0:T(8,128)(2,1)}, u32[]{:S(2)}) copy-start(bf16[2,3,4,4,16,512]{5,4,3,2,1,0:T(8,128)(2,1)} %param.5) | copy-start | bytes 4718596
  2.1 1.0 %copy-start.1 = (f32[2,2,3,3,4,4,16]{6,5,4,3,2,1,0:T(4,128)S(1)}, f32[2,2,3,3,4,4,16]{6,5,4,3,2,1,0:T(4,128)}, u32[]{:S(2)}) copy-start(f32[2,2,3,3,4,4,16]{6,5,4,3,2,1,0:T(4,128)} %param.6) | copy-start | bytes 110596
  3.0 58.1 %copy-start.2 = (bf16[2,8,2048]{2,1,0:T(8,128)(2,1)S(1)}, bf16[2,8,2048]{2,1,0:T(8,128)(2,1)}, u32[]{:S(2)}) copy-start(bf16[2,8,2048]{2,1,0:T(8,128)(2,1)} %peram.1) | copy-start | bytes 196612

commit v3 on v2

--- a/solution.py
+++ b/solution.py
@@ -18,7 +18,7 @@
     return (((y % 2) * NZ_RING + z) * CORES + core, x * 2 + y // 2)
 
 
-def reduce_kernel(norm, ev_in, links_in, out, ev, links, vt, right, face_f, face, halo_y, halo_yf, halo_x, send0, own, recv0,
+def reduce_kernel(norm, ev_in, links_in, out, ev, links, vt, right, face_f, face, halo_y, halo_x, send0, own, other, recv0,
                   send1, recv1, own2, send2, recv2, own3, send3, recv3, done3,
                   load, halo_send, halo_recv, core_send, core_recv, ring_send, ring_recv, z_send, z_recv):
     gx, gy = lax.axis_index("gx"), lax.axis_index("gy")
@@ -50,17 +50,32 @@
     for peer in peers:
         pl.semaphore_signal(barrier, inc=1, device_id=peer, device_id_type=MESH)
 
-    planes = ev.shape[2]
-
-    def take_face(s, carry):
+    nz, nx, ny, vecs = ev.shape[2:]
+    planes = nz * nx
+    inner, edge_x = 6 * nz * (nx - 1) * ny, 6 * nz * ny
+    main = inner + edge_x
+    faces = 6 * planes
+    loads[0].wait()
+
+    def take_faces(zz, carry):
         for p in range(2):
             for c in range(3):
-                face_f[pl.ds((p * 3 + c) * planes + s, 1), :] = ev[p, c, s].astype(F32)[0:1, :]
+                for xx in range(nx):
+                    value = ev[p, c, zz, xx].astype(F32)
+                    row = pl.ds((p * 3 + c) * planes + zz * nx + xx, 1)
+                    face_f[0, row, :] = value[0:1, :]
+                    face_f[1, row, :] = value[ny - 1 : ny, :]
         return carry
 
-    loads[0].wait()
-    lax.fori_loop(0, planes, take_face, 0)
-    face[...] = face_f[...].astype(BF16)
+    lax.fori_loop(0, nz, take_faces, 0)
+    face[...] = face_f[0].astype(BF16)
+
+    vt[:, :inner] = ev[:, :, :, : nx - 1].reshape(inner, vecs).T
+    vt[:, inner:main] = ev[:, :, :, nx - 1].reshape(edge_x, vecs).T
+    pad = jnp.zeros((vt.shape[1] - main - faces, vecs), F32)
+    vt[:, main:] = jnp.concatenate([face_f[1], pad], axis=0).T.astype(BF16)
+    for q in range(2):
+        right[0, q, main + faces :, :] = pad.astype(BF16)
     pl.semaphore_wait(barrier, len(peers))
 
     started = []
@@ -74,19 +89,14 @@
         return copy
 
     copy_y = send(face, halo_y, halo_send.at[0], halo_recv.at[0], before_y)
-    nz = planes // 4
-    copies_x = []
-    for zz in range(nz):
-        copies_x.append(
-            send(ev_in.at[:, :, zz * 4], halo_x.at[:, :, zz], halo_send.at[1 + zz], halo_recv.at[1 + zz], before_x)
-        )
-
-    vt[...] = ev[...].reshape(-1, ev.shape[-1]).T
-
-    def colour(h, s, source):
-        cols = links[pl.ds((1 - h) * 18 * planes + s, 18, stride=planes), :].T
-        coef = [jnp.broadcast_to(cols[:, i : i + 1], (16, LANES)) for i in range(18)]
-        for lane in range(ev.shape[-1] // LANES):
+    copies_x = [
+        send(ev_in.at[:, :, zz, 0], halo_x.at[:, :, zz], halo_send.at[1 + zz], halo_recv.at[1 + zz], before_x)
+        for zz in range(nz)
+    ]
+
+    def colour(h, columns, source, row_of):
+        coef = [jnp.broadcast_to(column, (column.shape[0], LANES)) for column in columns]
+        for lane in range(vecs // LANES):
             at = slice(lane * LANES, (lane + 1) * LANES)
             v = [[source(p, c, at) for c in range(3)] for p in range(2)]
             for a in range(3):
@@ -98,34 +108,92 @@
                     re = t_re if re is None else re + t_re
                     im = t_im if im is None else im + t_im
                 re, im = re.astype(BF16), im.astype(BF16)
-                right[h, 0, 0, a, s, :, at] = re
-                right[h, 0, 1, a, s, :, at] = im
-                right[h, 1, 0, a, s, :, at] = im
-                right[h, 1, 1, a, s, :, at] = -re
-
-    def gram(h, q):
-        lhs = vt[...]
-        wide = 2 * LANES
-        for j in range(ev.shape[-1] // wide):
-            rhs = right[h, q, :, :, :, :, j * wide : (j + 1) * wide].reshape(-1, wide)
-            yield j, jnp.dot(lhs, rhs, preferred_element_type=F32) * norm
-
-    rows = ev.shape[-1]
-
-    def gram_other(h):
-        for j, value in gram(h, 1 - core):
+                right[h, 0, row_of(0, a), at] = re
+                right[h, 0, row_of(1, a), at] = im
+                right[h, 1, row_of(0, a), at] = im
+                right[h, 1, row_of(1, a), at] = -re
+
+    def plane_columns(h, zz, xx):
+        columns = links[pl.ds((1 - h) * 18 * planes + zz * nx + xx, 18, stride=planes), :].T
+        return [columns[:, i : i + 1] for i in range(18)]
+
+    def plane_rows(zz, xx):
+        def row_of(p, c):
+            if xx < nx - 1:
+                start = (((p * 3 + c) * nz + zz) * (nx - 1) + xx) * ny
+            else:
+                start = inner + ((p * 3 + c) * nz + zz) * ny
+            return pl.ds(pl.multiple_of(start, ny), ny)
+
+        return row_of
+
+    def hop_x_inner(zz, carry):
+        for xx in range(nx - 1):
+            colour(1, plane_columns(1, zz, xx), lambda p, c, at: ev[p, c, zz, xx + 1, :, at].astype(F32),
+                   plane_rows(zz, xx))
+        return carry
+
+    def hop_x_last():
+        for zz in range(nz):
+            colour(1, plane_columns(1, zz, nx - 1), lambda p, c, at: halo_x[p, c, zz, :, at].astype(F32),
+                   plane_rows(zz, nx - 1))
+
+    def hop_y_main(zz, carry):
+        last = lax.broadcasted_iota(jnp.int32, (ny, LANES), 0) == ny - 1
+        for xx in range(nx):
+            def source(p, c, at):
+                return jnp.where(last, 0.0, pltpu.roll(ev[p, c, zz, xx, :, at].astype(F32), ny - 1, 0))
+
+            colour(0, plane_columns(0, zz, xx), source, plane_rows(zz, xx))
+        return carry
+
+    def hop_y_edge():
+        first_row = 18 * planes
+        columns = [links[first_row + i * planes : first_row + (i + 1) * planes, ny - 1 : ny] for i in range(18)]
+
+        def row_of(p, c):
+            start = main + (p * 3 + c) * planes
+            return slice(start, start + planes)
+
+        def source(p, c, at):
+            return halo_y[(p * 3 + c) * planes : (p * 3 + c + 1) * planes, at].astype(F32)
+
+        colour(0, columns, source, row_of)
+
+    def gram(h, q, low, high):
+        lhs = vt[:, low:high]
+        for j in range(vecs // (2 * LANES)):
+            rhs = right[h, q, low:high, j * 2 * LANES : (j + 1) * 2 * LANES]
+            value = jnp.dot(lhs, rhs, preferred_element_type=F32) * norm
             for half in range(2):
-                send0[h, (2 * j + half) * rows : (2 * j + half + 1) * rows, :] = value[
-                    :, half * LANES : (half + 1) * LANES
-                ].astype(BF16)
+                yield slice((2 * j + half) * vecs, (2 * j + half + 1) * vecs), value[:, half * LANES : (half + 1) * LANES]
+
+    def gram_x_inner():
+        for at, value in gram(1, 1 - core, 0, inner):
+            other[at, :] = value
+        for at, value in gram(1, core, 0, inner):
+            own[1, at, :] = value
+
+    def to_core(h):
         return send(send0.at[h], recv0.at[h], core_send.at[h, 0], core_recv.at[h, 0], sibling)
 
-    def gram_own(h):
-        for j, value in gram(h, core):
-            for half in range(2):
-                own[h, (2 * j + half) * rows : (2 * j + half + 1) * rows, :] = value[
-                    :, half * LANES : (half + 1) * LANES
-                ]
+    def gram_x_other():
+        for at, value in gram(1, 1 - core, inner, main):
+            send0[1, at, :] = (other[at, :] + value).astype(BF16)
+        return to_core(1)
+
+    def gram_x_own():
+        for at, value in gram(1, core, inner, main):
+            own[1, at, :] += value
+
+    def gram_y_other():
+        for at, value in gram(0, 1 - core, 0, vt.shape[1]):
+            send0[0, at, :] = value.astype(BF16)
+        return to_core(0)
+
+    def gram_y_own():
+        for at, value in gram(0, core, 0, vt.shape[1]):
+            own[0, at, :] = value
 
     first = ((x, at_x), (y, at_y))
     second = ((y, at_y), (x, at_x))
@@ -243,46 +311,24 @@
                 across.append(to_sibling(h, s, d, place))
         return across
 
-    def hop_x_inner(zz, carry):
-        for xx in range(3):
-            s = zz * 4 + xx
-            colour(1, s, lambda p, c, at: ev[p, c, s + 1, :, at].astype(F32))
-        return carry
-
-    def hop_x_last(zz, carry):
-        colour(1, zz * 4 + 3, lambda p, c, at: halo_x[p, c, zz, :, at].astype(F32))
-        return carry
-
-    def hop_y(s, carry):
-        last = lax.broadcasted_iota(jnp.int32, (16, LANES), 0) == 15
-        edges = [halo_yf[j, pl.ds(s, 6, stride=planes), :] for j in range(halo_yf.shape[0])]
-
-        def source(p, c, at):
-            value = pltpu.roll(ev[p, c, s, :, at].astype(F32), 15, 0)
-            edge = edges[at.start // LANES][p * 3 + c : p * 3 + c + 1, :]
-            return jnp.where(last, jnp.broadcast_to(edge, value.shape), value)
-
-        colour(0, s, source)
-        return carry
-
     loads[1].wait()
     lax.fori_loop(0, nz, hop_x_inner, 0)
-    copy_y.wait_recv()
-    for j in range(halo_yf.shape[0]):
-        halo_yf[j] = halo_y[:, j * LANES : (j + 1) * LANES].astype(F32)
-    lax.fori_loop(0, planes, hop_y, 0)
-    a = gram_other(0)
-    gram_own(0)
-    a = start1(0, a)
+    gram_x_inner()
+    lax.fori_loop(0, nz, hop_y_main, 0)
     for copy in copies_x:
         copy.wait_recv()
-    lax.fori_loop(0, nz, hop_x_last, 0)
-    b = gram_other(1)
-    gram_own(1)
-    b = start1(1, b)
+    hop_x_last()
+    a = gram_x_other()
+    gram_x_own()
+    copy_y.wait_recv()
+    hop_y_edge()
+    b = gram_y_other()
+    a = start1(1, a)
+    gram_y_own()
+    b = start1(0, b)
     for step in (start2, start3, gather3, gather2, gather1, gather0):
-        a = step(0, a)
-        b = step(1, b)
+        a = step(1, a)
+        b = step(0, b)
     for copy in a + b:
         copy.wait_recv()
     for copy in started:
@@ -327,12 +373,12 @@
     reim, colours, nz, nx, ny, vecs = eigen_vecs.shape
     sites = nz * nx * ny * lax.axis_size("gx") * lax.axis_size("gy")
     norm = 1.0 / math.sqrt(3.0 * sites)
-    planes = nz * nx
-    ev = eigen_vecs.reshape(reim, colours, planes, ny, vecs)
+    ev = eigen_vecs
     links = gauge_links.reshape(-1, ny)
     half = vecs * vecs // LANES
     vmem = pl.BlockSpec(memory_space=pltpu.VMEM)
-    faces = reim * colours * planes
+    faces = reim * colours * nz * nx
+    summed = faces * ny + -(-faces // LANES) * LANES
     g = pl.pallas_call(
         lambda *refs: reduce_kernel(norm, *refs),
         out_shape=jax.ShapeDtypeStruct((2, 2 * half, LANES), BF16),
@@ -341,15 +387,15 @@
         scratch_shapes=[
             pltpu.VMEM(ev.shape, BF16),
             pltpu.VMEM(links.shape, F32),
-            pltpu.VMEM((vecs, reim * colours * planes * ny), BF16),
-            pltpu.VMEM((2, 2, reim, colours, planes, ny, vecs), BF16),
-            pltpu.VMEM((faces, vecs), F32),
+            pltpu.VMEM((vecs, summed), BF16),
+            pltpu.VMEM((2, 2, summed, vecs), BF16),
+            pltpu.VMEM((2, faces, vecs), F32),
             pltpu.VMEM((faces, vecs), BF16),
             pltpu.VMEM((faces, vecs), BF16),
-            pltpu.VMEM((vecs // LANES, faces, LANES), F32),
             pltpu.VMEM((reim, colours, nz, ny, vecs), BF16),
             pltpu.VMEM((2, half, LANES), BF16),
             pltpu.VMEM((2, half, LANES), F32),
+            pltpu.VMEM((half, LANES), F32),
             pltpu.VMEM((2, half, LANES), BF16),
             pltpu.VMEM((2, half, LANES), BF16),
             pltpu.VMEM((2, 2, 3, half // 8, LANES), BF16),

time: 63.7 us -> 60.3 us (0.947)
  Pallas kernels: 60.5 us -> 57.1 us
    pallas_call x1, Pallas kernels: 58 us -> 54.6 us  [local(): pl.pallas_call(lambda *refs: reduce_kernel(norm, *refs), out_shape=jax.Sh...]
where the time goes in v3:
time: 60.3 us; the launch traced here: 60.1 us
  Pallas kernels  57.1 us (95%)
  local copies, waits for them, and re-layouts  2.39 us (4%)
  between operations  0.69 us (1%)
    pallas_call x1, Pallas kernels, local(): pl.pallas_call(lambda *refs: reduce_kernel(norm, *refs), out_shape=jax.Sh...  54.6 us
    pallas_call x1, Pallas kernels, local(): pl.pallas_call(contract_kernel, out_shape=(jax.ShapeDtypeStruct((4, 2, ow...  2.47 us
    unnamed x10, local copies, waits for them, and re-layouts  2.39 us

profile of v3, /device:TPU:1, one launch (start us, length us, event | category | flops | bytes accessed | tf_op | source)
XLA Modules:
  0.0 60.1 jit_solution(3487836233088190483)
XLA Ops:
  0.6 0.0 copy-start.4
  0.6 0.0 copy-start.3
  0.7 0.0 copy-start
  0.7 1.4 %copy-done = bf16[2,3,4,4,16,512]{5,4,3,2,1,0:T(8,128)(2,1)S(1)} copy-done((bf16[2,3,4,4,16,512]{5,4,3,2,1,0:T(8,128)(2,1)S(1)}, bf16[2,3,4,4,16,512]{5,4,3,2,1,0:T(8,128)(2,1)}, u32[]{:S(2)}) %copy-start) | copy-done | bytes 1572888
  2.1 0.0 copy-start.1
  2.1 1.0 %copy-done.1 = f32[2,2,3,3,4,4,16]{6,5,4,3,2,1,0:T(4,128)S(1)} copy-done((f32[2,2,3,3,4,4,16]{6,5,4,3,2,1,0:T(4,128)S(1)}, f32[2,2,3,3,4,4,16]{6,5,4,3,2,1,0:T(4,128)}, u32[]{:S(2)}) %copy-start.1) | copy-done | bytes 36888
  3.0 0.0 copy-start.2
  3.0 54.6 %reduce.1.g = bf16[2,4096,128]{2,1,0:T(8,128)(2,1)S(1)} custom-call(bf16[2,3,4,4,16,512]{5,4,3,2,1,0:T(8,128)(2,1)S(1)} %copy-done, f32[576,16]{1,0:T(8,128)S(1)} %bitcast.1), custom_call_target="tpu_custom_call" | custom-call | tf_op jit(solution)/shard_map/reduce/pallas_call | solution.py:382
  57.6 0.0 copy-done.4
  57.6 0.0 copy-done.3
  57.6 0.0 copy-done.2
  57.7 2.5 %contract.1 = (f32[4,2,16,512]{3,2,1,0:T(8,128)}, bf16[4,2,8,2048]{3,2,1,0:T(8,128)(2,1)}) custom-call(s32[4]{0:T(128)S(1)} %copy-done.3, s32[4]{0:T(128)S(1)} %copy-done.4, bf16[2,4096,128]{2,1,0:T(8,128)(2,1)S(1)} %reduce.1.g, bf16[2,8,2048]{2,1,0:T(8,128)(2,1)S(1)} %copy-done.2), custom_call_target="tpu_custom_call" | custom-call | tf_op jit(solution)/shard_map/contract/pallas_call | solution.py:427
Async XLA Ops:
  0.6 57.0 %copy-start.4 = (s32[4]{0:T(128)S(1)}, s32[4]{0:T(128)}, u32[]{:S(2)}) copy-start(s32[4]{0:T(128)} %spins.1) | copy-start | bytes 52
  0.6 57.0 %copy-start.3 = (s32[4]{0:T(128)S(1)}, s32[4]{0:T(128)}, u32[]{:S(2)}) copy-start(s32[4]{0:T(128)} %directions.1) | copy-start | bytes 52
  0.7 1.4 %copy-start = (bf16[2,3,4,4,16,512]{5,4,3,2,1,0:T(8,128)(2,1)S(1)}, bf16[2,3,4,4,16,512]{5,4,3,2,1,0:T(8,128)(2,1)}, u32[]{:S(2)}) copy-start(bf16[2,3,4,4,16,512]{5,4,3,2,1,0:T(8,128)(2,1)} %refs_0_.1) | copy-start | bytes 4718596
  2.1 1.0 %copy-start.1 = (f32[2,2,3,3,4,4,16]{6,5,4,3,2,1,0:T(4,128)S(1)}, f32[2,2,3,3,4,4,16]{6,5,4,3,2,1,0:T(4,128)}, u32[]{:S(2)}) copy-start(f32[2,2,3,3,4,4,16]{6,5,4,3,2,1,0:T(4,128)} %param.6) | copy-start | bytes 110596
  3.0 54.6 %copy-start.2 = (bf16[2,8,2048]{2,1,0:T(8,128)(2,1)S(1)}, bf16[2,8,2048]{2,1,0:T(8,128)(2,1)}, u32[]{:S(2)}) copy-start(bf16[2,8,2048]{2,1,0:T(8,128)(2,1)} %peram.1) | copy-start | bytes 196612

commit v4 on v3

--- a/solution.py
+++ b/solution.py
@@ -18,9 +18,9 @@
     return (((y % 2) * NZ_RING + z) * CORES + core, x * 2 + y // 2)
 
 
-def reduce_kernel(norm, ev_in, links_in, out, ev, links, vt, right, face_f, face, halo_y, halo_x, send0, own, other, recv0,
-                  send1, recv1, own2, send2, recv2, own3, send3, recv3, done3,
-                  load, halo_send, halo_recv, core_send, core_recv, ring_send, ring_recv, z_send, z_recv):
+def reduce_kernel(norm, ev_in, links_in, peram_in, parts, picks, products, out, ev, links, peram, lhs_f, lhs, vt, right, face_f, face, halo_y, halo_x, send0, own, other, recv0,
+                  send1, recv1, own2, send2, recv2, own3, send3, recv3, done3, there,
+                  load, peram_send, peram_recv, halo_send, halo_recv, core_send, core_recv, ring_send, ring_recv, z_send, z_recv):
     gx, gy = lax.axis_index("gx"), lax.axis_index("gy")
     core, z = gx % 2, (gx // 2) % NZ_RING
     x, y = gy // 2, (gy % 2) * 2 + gx // (2 * NZ_RING)
@@ -39,7 +39,11 @@
     before_x, after_x = ((gx + n_gx - 1) % n_gx, gy), ((gx + 1) % n_gx, gy)
     before_y, after_y = (gx, (gy + n_gy - 1) % n_gy), (gx, (gy + 1) % n_gy)
 
-    loads = [pltpu.make_async_copy(ev_in, ev, load.at[0]), pltpu.make_async_copy(links_in, links, load.at[1])]
+    loads = [
+        pltpu.make_async_copy(ev_in, ev, load.at[0]),
+        pltpu.make_async_copy(links_in, links, load.at[1]),
+        pltpu.make_async_copy(peram_in, peram.at[0], load.at[2]),
+    ]
     for copy in loads:
         copy.start()
     barrier = pltpu.get_barrier_semaphore()
@@ -93,6 +97,8 @@
         send(ev_in.at[:, :, zz, 0], halo_x.at[:, :, zz], halo_send.at[1 + zz], halo_recv.at[1 + zz], before_x)
         for zz in range(nz)
     ]
+
+    copy_p = send(peram_in, peram.at[1], peram_send, peram_recv, sibling)
 
     def colour(h, columns, source, row_of):
         coef = [jnp.broadcast_to(column, (column.shape[0], LANES)) for column in columns]
@@ -123,7 +129,7 @@
                 start = (((p * 3 + c) * nz + zz) * (nx - 1) + xx) * ny
             else:
                 start = inner + ((p * 3 + c) * nz + zz) * ny
-            return pl.ds(pl.multiple_of(start, ny), ny)
+            return slice(start, start + ny) if isinstance(start, int) else pl.ds(pl.multiple_of(start, ny), ny)
 
         return row_of
 
@@ -251,7 +257,7 @@
         ]
 
     def base(s):
-        b0 = core * half + s * part
+        b0 = s * part
         b1 = b0 + first[s][0] * len1
         return b0, b1, b1 + second[s][0] * len2
 
@@ -284,89 +290,100 @@
             ]
         return result
 
-    def to_sibling(h, s, d, place):
-        return send(out.at[h, place], out.at[h, place], core_send.at[h, 1 + 4 * s + d], core_recv.at[h, 1 + 4 * s + d],
-                    sibling)
-
     def gather1(h, copies):
         for copy in copies:
             copy.wait_recv()
-        rings, across = [], []
+        result = []
         for s in range(2):
             place = pl.ds(base(s)[1], len1)
-            rings.append([
+            result += [
                 send(out.at[h, place], out.at[h, place], ring_send.at[h, 3, s, d - 1], ring_recv.at[h, 3, s, d - 1],
                      first[s][1](d))
                 for d in range(1, 4)
-            ])
-            across.append(to_sibling(h, s, 0, place))
-        return rings, across
-
-    def gather0(h, both):
-        rings, across = both
-        for d in (1, 3, 2):
-            for s in range(2):
-                rings[s][d - 1].wait_recv()
-                place = pl.ds(base(s)[0] + (first[s][0] + 4 - d) % 4 * len1, len1)
-                across.append(to_sibling(h, s, d, place))
-        return across
+            ]
+        return result
+
+    m = lhs.shape[1] - vecs // n_gx
+    own_rows = lhs.shape[1] - m
+
+    def make_lhs():
+        rows = peram.shape[2]
+        for who in range(2):
+            place = gx if who == 0 else gx + 1 - 2 * core
+            for p in range(2):
+                value = peram[who, p].astype(F32)
+                for t in range(4):
+                    start = (p * 4 + t) * rows
+                    lhs_f[who, start : start + rows, :] = value[:, t * vecs : (t + 1) * vecs]
+            column = lax.broadcasted_iota(jnp.int32, (own_rows, vecs), 1)
+            row = lax.broadcasted_iota(jnp.int32, (own_rows, vecs), 0)
+            lhs_f[who, m:, :] = jnp.where(column == place * own_rows + row, 1.0, 0.0)
+        lhs[...] = lhs_f[...].astype(BF16)
+
+    def contract(h, copies):
+        for copy in copies:
+            copy.wait_recv()
+        blocks = out.shape[1] // vecs
+        value = jnp.concatenate([out[h, j * vecs : (j + 1) * vecs, :] for j in range(blocks)], axis=1)
+        across = (((1,), (1,)), ((), ()))
+        there[h, 0] = jnp.dot(lhs[1], value, preferred_element_type=F32)
+        there[h, 1] = lax.dot_general(lhs[1], value, across, preferred_element_type=F32)
+        copy = send(there.at[h], products.at[core, h], core_send.at[h, 1], core_recv.at[h, 1], sibling)
+        products[core, h, 0] = jnp.dot(lhs[0], value, preferred_element_type=F32)
+        products[core, h, 1] = lax.dot_general(lhs[0], value, across, preferred_element_type=F32)
+        return [copy]
+
+    def combine(h, copies):
+        copies[0].wait_recv()
+        low = m // 2
+        re, im = products[0, h, 0], products[1, h, 0]
+        parts[h, 0] = (re[:low] - im[low:m]).astype(BF16)
+        parts[h, 1] = (im[:low] + re[low:m]).astype(BF16)
+        picks[h, 0] = re[m:]
+        picks[h, 1] = im[m:]
+        re, im = products[0, h, 1], products[1, h, 1]
+        parts[2 + h, 0] = (re[:low] + im[low:m]).astype(BF16)
+        parts[2 + h, 1] = (re[low:m] - im[:low]).astype(BF16)
+        picks[2 + h, 0] = re[m:]
+        picks[2 + h, 1] = -im[m:]
 
     loads[1].wait()
-    lax.fori_loop(0, nz, hop_x_inner, 0)
+    for zz in range(nz):
+        hop_x_inner(zz, 0)
     gram_x_inner()
-    lax.fori_loop(0, nz, hop_y_main, 0)
+    for zz in range(nz):
+        hop_y_main(zz, 0)
+    copy_y.wait_recv()
+    hop_y_edge()
+    b = gram_y_other()
     for copy in copies_x:
         copy.wait_recv()
     hop_x_last()
     a = gram_x_other()
-    gram_x_own()
-    copy_y.wait_recv()
-    hop_y_edge()
-    b = gram_y_other()
-    a = start1(1, a)
     gram_y_own()
     b = start1(0, b)
-    for step in (start2, start3, gather3, gather2, gather1, gather0):
+    gram_x_own()
+    a = start1(1, a)
+    loads[2].wait()
+    copy_p.wait_recv()
+    make_lhs()
+    for step in (start2, start3, gather3, gather2, gather1, contract):
+        b = step(0, b)
         a = step(1, a)
-        b = step(0, b)
-    for copy in a + b:
-        copy.wait_recv()
+    combine(0, b)
+    combine(1, a)
     for copy in started:
         copy.wait_send()
 
 
-def contract_kernel(directions, spins, g, peram, elementals, contracted, products):
-    gx = lax.axis_index("gx")
-    vecs = peram.shape[-1] // 4
-    rows = peram.shape[1]
-    own_rows = elementals.shape[2]
-    pieces = [peram[p].astype(F32)[:, t * vecs : (t + 1) * vecs] for p in range(2) for t in range(4)]
-    pick = lax.broadcasted_iota(jnp.int32, (own_rows, vecs), 1) == gx * own_rows + lax.broadcasted_iota(
-        jnp.int32, (own_rows, vecs), 0
-    )
-    lhs = jnp.concatenate(pieces + [jnp.where(pick, 1.0, 0.0)], axis=0).astype(BF16)
-    m = 4 * rows
-    for h in range(2):
-        parts = []
-        for q in range(2):
-            blocks = [g[h, (q * 4 + j) * vecs : (q * 4 + j + 1) * vecs, :] for j in range(4)]
-            parts.append(jnp.concatenate(blocks, axis=1))
-        re = jnp.dot(lhs, parts[0], preferred_element_type=F32)
-        im = jnp.dot(lhs, parts[1], preferred_element_type=F32)
-        products[h, 0] = jnp.concatenate([re[:m] - im[m : 2 * m], re[2 * m :]], 0)
-        products[h, 1] = jnp.concatenate([im[:m] + re[m : 2 * m], im[2 * m :]], 0)
-        over = (((1,), (1,)), ((), ()))
-        re = lax.dot_general(lhs, parts[0], over, preferred_element_type=F32)
-        im = lax.dot_general(lhs, parts[1], over, preferred_element_type=F32)
-        products[2 + h, 0] = jnp.concatenate([re[:m] + im[m : 2 * m], re[2 * m :]], 0)
-        products[2 + h, 1] = jnp.concatenate([re[m : 2 * m] - im[:m], -im[2 * m :]], 0)
+def place_kernel(directions, spins, parts, picks, elementals, contracted):
+    rows, vecs = contracted.shape[2], elementals.shape[3]
     for k in range(4):
         which = jnp.where(directions[k] % 2 == 0, directions[k] + 1, directions[k] - 1)
+        elementals[k] = picks[which]
         for q in range(2):
-            elementals[k, q] = products[which, q, m : m + own_rows, :]
             for u in range(4):
-                row = pl.multiple_of(spins[u] * rows, rows)
-                contracted[k, q, :, u * vecs : (u + 1) * vecs] = products[which, q, pl.ds(row, rows), :].astype(BF16)
+                contracted[k, q, :, u * vecs : (u + 1) * vecs] = parts[which, q, spins[u]]
 
 
 def local(eigen_vecs, gauge_links, directions, spin_map, perambulator):
@@ -379,14 +396,25 @@
     vmem = pl.BlockSpec(memory_space=pltpu.VMEM)
     faces = reim * colours * nz * nx
     summed = faces * ny + -(-faces // LANES) * LANES
-    g = pl.pallas_call(
+    rows = perambulator.shape[1]
+    own_rows = vecs // lax.axis_size("gx")
+    lhs_rows = 8 * rows + own_rows
+    parts, picks = pl.pallas_call(
         lambda *refs: reduce_kernel(norm, *refs),
-        out_shape=jax.ShapeDtypeStruct((2, 2 * half, LANES), BF16),
-        in_specs=[pl.BlockSpec(memory_space=pltpu.HBM)] * 2,
-        out_specs=vmem,
+        out_shape=(
+            jax.ShapeDtypeStruct((4, 2, 4 * rows, vecs), BF16),
+            jax.ShapeDtypeStruct((4, 2, own_rows, vecs), F32),
+        ),
+        in_specs=[pl.BlockSpec(memory_space=pltpu.HBM)] * 3,
+        out_specs=(vmem, vmem),
         scratch_shapes=[
+            pltpu.VMEM((2, 2, 2, lhs_rows, vecs), F32),
+            pltpu.VMEM((2, half, LANES), BF16),
             pltpu.VMEM(ev.shape, BF16),
             pltpu.VMEM(links.shape, F32),
+            pltpu.VMEM((2, *perambulator.shape), BF16),
+            pltpu.VMEM((2, lhs_rows, vecs), F32),
+            pltpu.VMEM((2, lhs_rows, vecs), BF16),
             pltpu.VMEM((vecs, summed), BF16),
             pltpu.VMEM((2, 2, summed, vecs), BF16),
             pltpu.VMEM((2, faces, vecs), F32),
@@ -406,36 +434,36 @@
             pltpu.VMEM((2, half // 16, LANES), BF16),
             pltpu.VMEM((2, NZ_RING - 1, half // 128, LANES), BF16),
             pltpu.VMEM((2, half // 16, LANES), BF16),
-            pltpu.SemaphoreType.DMA((2,)),
+            pltpu.VMEM((2, 2, lhs_rows, vecs), F32),
+            pltpu.SemaphoreType.DMA((3,)),
+            pltpu.SemaphoreType.DMA,
+            pltpu.SemaphoreType.DMA,
             pltpu.SemaphoreType.DMA((1 + nz,)),
             pltpu.SemaphoreType.DMA((1 + nz,)),
-            pltpu.SemaphoreType.DMA((2, 9)),
-            pltpu.SemaphoreType.DMA((2, 9)),
+            pltpu.SemaphoreType.DMA((2, 2)),
+            pltpu.SemaphoreType.DMA((2, 2)),
             pltpu.SemaphoreType.DMA((2, 4, 2, 3)),
             pltpu.SemaphoreType.DMA((2, 4, 2, 3)),
             pltpu.SemaphoreType.DMA((2, 2, NZ_RING - 1)),
             pltpu.SemaphoreType.DMA((2, 2, NZ_RING - 1)),
         ],
         compiler_params=pltpu.CompilerParams(
-            collective_id=0, has_side_effects=True, vmem_limit_bytes=48 * 2**20
+            collective_id=0, has_side_effects=True, vmem_limit_bytes=int(53.35 * 2**20)
         ),
         name="reduce",
-    )(ev, links)
-    rows = perambulator.shape[1]
-    own_rows = vecs // lax.axis_size("gx")
+    )(ev, links, perambulator)
     smem = pl.BlockSpec(memory_space=pltpu.SMEM)
     return pl.pallas_call(
-        contract_kernel,
+        place_kernel,
         out_shape=(
             jax.ShapeDtypeStruct((4, 2, own_rows, vecs), F32),
             jax.ShapeDtypeStruct((4, 2, rows, 4 * vecs), BF16),
         ),
         in_specs=[smem, smem, vmem, vmem],
         out_specs=(vmem, vmem),
-        scratch_shapes=[pltpu.VMEM((4, 2, 4 * rows + own_rows, vecs), F32)],
         compiler_params=pltpu.CompilerParams(vmem_limit_bytes=32 * 2**20),
-        name="contract",
-    )(directions, spin_map, g, perambulator)
+        name="place",
+    )(directions, spin_map, parts.reshape(4, 2, 4, rows, vecs), picks)
 
 
 def solution(mesh):

time: 60.3 us -> 57.4 us (0.952)
  local copies, waits for them, and re-layouts: 2.39 us -> 0.85 us
  Pallas kernels: 57.1 us -> 55.7 us
    unnamed x10 -> x6, local copies, waits for them, and re-layouts: 2.39 us -> 0.85 us
    pallas_call x2, Pallas kernels: 57.1 us -> 55.7 us  [the longest x1 54.3 us: local(): pl.pallas_call(lambda *refs: reduce_kernel(norm, *refs), out_shape=(jax.S...]
where the time goes in v4:
time: 57.4 us; the launch traced here: 57.2 us
  Pallas kernels  55.7 us (97%)
  local copies, waits for them, and re-layouts  0.85 us (1%)
  between operations  0.68 us (1%)
    pallas_call x1, Pallas kernels, local(): pl.pallas_call(lambda *refs: reduce_kernel(norm, *refs), out_shape=(jax.S...  54.3 us
    pallas_call x1, Pallas kernels, local(): pl.pallas_call(place_kernel, out_shape=(jax.ShapeDtypeStruct((4, 2, own_r...  1.38 us

profile of v4, /device:TPU:1, one launch (start us, length us, event | category | flops | bytes accessed | tf_op | source)
XLA Modules:
  0.0 57.2 jit_solution(17688062550676430286)
XLA Ops:
  0.6 0.0 copy-start.2
  0.6 0.0 copy-start.1
  0.7 0.0 copy-start
  0.7 0.8 %copy-done = bf16[2,8,2048]{2,1,0:T(8,128)(2,1)S(1)} copy-done((bf16[2,8,2048]{2,1,0:T(8,128)(2,1)S(1)}, bf16[2,8,2048]{2,1,0:T(8,128)(2,1)}, u32[]{:S(2)}) %copy-start) | copy-done | bytes 65560
  1.5 54.3 %reduce.1 = (bf16[4,2,32,512]{3,2,1,0:T(8,128)(2,1)S(1)}, f32[4,2,16,512]{3,2,1,0:T(8,128)S(1)}) custom-call(bf16[2,3,4,4,16,512]{5,4,3,2,1,0:T(8,128)(2,1)} %refs_0_.1, f32[576,16]{1,0:T(8,128)} %bitcast.3, bf16[2,8,2048]{2,1,0:T(8,128)(2,1)S(1)} %copy-done), custom_call_target="tpu_custom_call" | custom-call | tf_op jit(solution)/shard_map/reduce/pallas_call | solution.py:402
  55.8 0.0 copy-done.2
  55.8 0.0 copy-done.1
  55.8 1.4 %place.1 = (f32[4,2,16,512]{3,2,1,0:T(8,128)}, bf16[4,2,8,2048]{3,2,1,0:T(8,128)(2,1)}) custom-call(s32[4]{0:T(128)S(1)} %copy-done.1, s32[4]{0:T(128)S(1)} %copy-done.2, bf16[4,2,4,8,512]{4,3,2,1,0:T(8,128)(2,1)S(1)} %bitcast.2, f32[4,2,16,512]{3,2,1,0:T(8,128)S(1)} %get-tuple-element.5.picks), custom_call_target="tpu_custom_call" | custom-call | tf_op jit(solution)/shard_map/place/pallas_call | solution.py:456
Async XLA Ops:
  0.6 55.2 %copy-start.2 = (s32[4]{0:T(128)S(1)}, s32[4]{0:T(128)}, u32[]{:S(2)}) copy-start(s32[4]{0:T(128)} %spins.1) | copy-start | bytes 52
  0.6 55.2 %copy-start.1 = (s32[4]{0:T(128)S(1)}, s32[4]{0:T(128)}, u32[]{:S(2)}) copy-start(s32[4]{0:T(128)} %directions.1) | copy-start | bytes 52
  0.7 0.9 %copy-start = (bf16[2,8,2048]{2,1,0:T(8,128)(2,1)S(1)}, bf16[2,8,2048]{2,1,0:T(8,128)(2,1)}, u32[]{:S(2)}) copy-start(bf16[2,8,2048]{2,1,0:T(8,128)(2,1)} %refs_2_.1) | copy-start | bytes 196612

commit v5 on v4

--- a/solution.py
+++ b/solution.py
@@ -91,6 +91,10 @@
         copy.start()
         started.append(copy)
         return copy
+
+    def around(count, make):
+        made = {d: make(d) for d in sorted(range(1, count), key=lambda d: -min(d, count - d))}
+        return [made[d] for d in range(1, count)]
 
     copy_y = send(face, halo_y, halo_send.at[0], halo_recv.at[0], before_y)
     copies_x = [
@@ -180,22 +184,29 @@
         for at, value in gram(1, core, 0, inner):
             own[1, at, :] = value
 
-    def to_core(h):
-        return send(send0.at[h], recv0.at[h], core_send.at[h, 0], core_recv.at[h, 0], sibling)
+    def to_core(h, s):
+        mine = pl.ds(s * part, part)
+        return send(send0.at[h, mine], recv0.at[h, mine], core_send.at[h, s], core_recv.at[h, s], sibling)
 
     def gram_x_other():
-        for at, value in gram(1, 1 - core, inner, main):
+        copies = []
+        for n, (at, value) in enumerate(gram(1, 1 - core, inner, main)):
             send0[1, at, :] = (other[at, :] + value).astype(BF16)
-        return to_core(1)
+            if n % 2 == 1:
+                copies.append(to_core(1, n // 2))
+        return copies
 
     def gram_x_own():
         for at, value in gram(1, core, inner, main):
             own[1, at, :] += value
 
     def gram_y_other():
-        for at, value in gram(0, 1 - core, 0, vt.shape[1]):
+        copies = []
+        for n, (at, value) in enumerate(gram(0, 1 - core, 0, vt.shape[1])):
             send0[0, at, :] = value.astype(BF16)
-        return to_core(0)
+            if n % 2 == 1:
+                copies.append(to_core(0, n // 2))
+        return copies
 
     def gram_y_own():
         for at, value in gram(0, core, 0, vt.shape[1]):
@@ -206,19 +217,18 @@
     half = own.shape[1]
     part, len1, len2, len3 = half // 2, half // 8, half // 32, half // 256
 
-    def start1(h, copy):
-        copy.wait_recv()
-        total = own[h] + recv0[h].astype(F32)
-        own[h] = total
-        send1[h] = total.astype(BF16)
-        return [
-            [
-                send(send1.at[h, pl.ds(s * part + (first[s][0] + d) % 4 * len1, len1)], recv1.at[h, s, d - 1],
-                     ring_send.at[h, 0, s, d - 1], ring_recv.at[h, 0, s, d - 1], first[s][1](d))
-                for d in range(1, 4)
-            ]
-            for s in range(2)
-        ]
+    def start1(h, copies):
+        result = []
+        for s in range(2):
+            copies[s].wait_recv()
+            mine = pl.ds(s * part, part)
+            total = own[h, mine] + recv0[h, mine].astype(F32)
+            own[h, mine] = total
+            send1[h, mine] = total.astype(BF16)
+            result.append(around(4, lambda d: send(
+                send1.at[h, pl.ds(s * part + (first[s][0] + d) % 4 * len1, len1)], recv1.at[h, s, d - 1],
+                ring_send.at[h, 0, s, d - 1], ring_recv.at[h, 0, s, d - 1], first[s][1](d))))
+        return result
 
     def start2(h, copies):
         result = []
@@ -230,11 +240,9 @@
             own2[h, s] = total
             send2[h, s] = total.astype(BF16)
             place, at = second[s]
-            result.append([
-                send(send2.at[h, s, pl.ds((place + d) % 4 * len2, len2)], recv2.at[h, s, d - 1],
-                     ring_send.at[h, 1, s, d - 1], ring_recv.at[h, 1, s, d - 1], at(d))
-                for d in range(1, 4)
-            ])
+            result.append(around(4, lambda d: send(
+                send2.at[h, s, pl.ds((place + d) % 4 * len2, len2)], recv2.at[h, s, d - 1],
+                ring_send.at[h, 1, s, d - 1], ring_recv.at[h, 1, s, d - 1], at(d))))
         return result
 
     def start3(h, copies):
@@ -250,11 +258,9 @@
         )
         own3[h] = total
         send3[h] = total.astype(BF16)
-        return [
-            send(send3.at[h, pl.ds((z + d) % NZ_RING * 2 * len3, 2 * len3)], recv3.at[h, d - 1],
-                 z_send.at[h, 0, d - 1], z_recv.at[h, 0, d - 1], at_z(d))
-            for d in range(1, NZ_RING)
-        ]
+        return around(NZ_RING, lambda d: send(
+            send3.at[h, pl.ds((z + d) % NZ_RING * 2 * len3, 2 * len3)], recv3.at[h, d - 1],
+            z_send.at[h, 0, d - 1], z_recv.at[h, 0, d - 1], at_z(d)))
 
     def base(s):
         b0 = s * part
@@ -268,10 +274,8 @@
             copy.wait_recv()
             total = total + recv3[h, d].astype(F32)
         done3[h, place] = total.astype(BF16)
-        return [
-            send(done3.at[h, place], done3.at[h, place], z_send.at[h, 1, d - 1], z_recv.at[h, 1, d - 1], at_z(d))
-            for d in range(1, NZ_RING)
-        ]
+        return around(NZ_RING, lambda d: send(
+            done3.at[h, place], done3.at[h, place], z_send.at[h, 1, d - 1], z_recv.at[h, 1, d - 1], at_z(d)))
 
     def gather2(h, copies):
         for copy in copies:
@@ -283,11 +287,9 @@
             out[h, place] = jnp.concatenate(
                 [value[(2 * i + s) * len3 : (2 * i + s + 1) * len3] for i in range(NZ_RING)], axis=0
             ).astype(BF16)
-            result += [
-                send(out.at[h, place], out.at[h, place], ring_send.at[h, 2, s, d - 1], ring_recv.at[h, 2, s, d - 1],
-                     second[s][1](d))
-                for d in range(1, 4)
-            ]
+            result += around(4, lambda d: send(
+                out.at[h, place], out.at[h, place], ring_send.at[h, 2, s, d - 1], ring_recv.at[h, 2, s, d - 1],
+                second[s][1](d)))
         return result
 
     def gather1(h, copies):
@@ -296,11 +298,9 @@
         result = []
         for s in range(2):
             place = pl.ds(base(s)[1], len1)
-            result += [
-                send(out.at[h, place], out.at[h, place], ring_send.at[h, 3, s, d - 1], ring_recv.at[h, 3, s, d - 1],
-                     first[s][1](d))
-                for d in range(1, 4)
-            ]
+            result += around(4, lambda d: send(
+                out.at[h, place], out.at[h, place], ring_send.at[h, 3, s, d - 1], ring_recv.at[h, 3, s, d - 1],
+                first[s][1](d)))
         return result
 
     m = lhs.shape[1] - vecs // n_gx
@@ -328,7 +328,7 @@
         across = (((1,), (1,)), ((), ()))
         there[h, 0] = jnp.dot(lhs[1], value, preferred_element_type=F32)
         there[h, 1] = lax.dot_general(lhs[1], value, across, preferred_element_type=F32)
-        copy = send(there.at[h], products.at[core, h], core_send.at[h, 1], core_recv.at[h, 1], sibling)
+        copy = send(there.at[h], products.at[core, h], core_send.at[h, 2], core_recv.at[h, 2], sibling)
         products[core, h, 0] = jnp.dot(lhs[0], value, preferred_element_type=F32)
         products[core, h, 1] = lax.dot_general(lhs[0], value, across, preferred_element_type=F32)
         return [copy]
@@ -440,8 +440,8 @@
             pltpu.SemaphoreType.DMA,
             pltpu.SemaphoreType.DMA((1 + nz,)),
             pltpu.SemaphoreType.DMA((1 + nz,)),
-            pltpu.SemaphoreType.DMA((2, 2)),
-            pltpu.SemaphoreType.DMA((2, 2)),
+            pltpu.SemaphoreType.DMA((2, 3)),
+            pltpu.SemaphoreType.DMA((2, 3)),
             pltpu.SemaphoreType.DMA((2, 4, 2, 3)),
             pltpu.SemaphoreType.DMA((2, 4, 2, 3)),
             pltpu.SemaphoreType.DMA((2, 2, NZ_RING - 1)),

time: 57.4 us -> 56.9 us (level)
  no operation moved by 1% of the time
where the time goes in v5:
time: 56.9 us; the launch traced here: 56.7 us
  Pallas kernels  55.2 us (97%)
  local copies, waits for them, and re-layouts  0.85 us (1%)
  between operations  0.68 us (1%)
    pallas_call x1, Pallas kernels, local(): pl.pallas_call(lambda *refs: reduce_kernel(norm, *refs), out_shape=(jax.S...  53.8 us
    pallas_call x1, Pallas kernels, local(): pl.pallas_call(place_kernel, out_shape=(jax.ShapeDtypeStruct((4, 2, own_r...  1.38 us

profile of v5, /device:TPU:1, one launch (start us, length us, event | category | flops | bytes accessed | tf_op | source)
XLA Modules:
  0.0 56.7 jit_solution(9121347108298729428)
XLA Ops:
  0.6 0.0 copy-start.2
  0.6 0.0 copy-start.1
  0.7 0.0 copy-start
  0.7 0.8 %copy-done = bf16[2,8,2048]{2,1,0:T(8,128)(2,1)S(1)} copy-done((bf16[2,8,2048]{2,1,0:T(8,128)(2,1)S(1)}, bf16[2,8,2048]{2,1,0:T(8,128)(2,1)}, u32[]{:S(2)}) %copy-start) | copy-done | bytes 65560
  1.5 53.8 %reduce.1 = (bf16[4,2,32,512]{3,2,1,0:T(8,128)(2,1)S(1)}, f32[4,2,16,512]{3,2,1,0:T(8,128)S(1)}) custom-call(bf16[2,3,4,4,16,512]{5,4,3,2,1,0:T(8,128)(2,1)} %refs_0_.1, f32[576,16]{1,0:T(8,128)} %bitcast.3, bf16[2,8,2048]{2,1,0:T(8,128)(2,1)S(1)} %copy-done), custom_call_target="tpu_custom_call" | custom-call | tf_op jit(solution)/shard_map/reduce/pallas_call | solution.py:402
  55.3 0.0 copy-done.2
  55.3 0.0 copy-done.1
  55.3 1.4 %place.1 = (f32[4,2,16,512]{3,2,1,0:T(8,128)}, bf16[4,2,8,2048]{3,2,1,0:T(8,128)(2,1)}) custom-call(s32[4]{0:T(128)S(1)} %copy-done.1, s32[4]{0:T(128)S(1)} %copy-done.2, bf16[4,2,4,8,512]{4,3,2,1,0:T(8,128)(2,1)S(1)} %bitcast.2, f32[4,2,16,512]{3,2,1,0:T(8,128)S(1)} %get-tuple-element.5.picks), custom_call_target="tpu_custom_call" | custom-call | tf_op jit(solution)/shard_map/place/pallas_call | solution.py:456
Async XLA Ops:
  0.6 54.7 %copy-start.2 = (s32[4]{0:T(128)S(1)}, s32[4]{0:T(128)}, u32[]{:S(2)}) copy-start(s32[4]{0:T(128)} %spins.1) | copy-start | bytes 52
  0.6 54.7 %copy-start.1 = (s32[4]{0:T(128)S(1)}, s32[4]{0:T(128)}, u32[]{:S(2)}) copy-start(s32[4]{0:T(128)} %directions.1) | copy-start | bytes 52
  0.7 0.9 %copy-start = (bf16[2,8,2048]{2,1,0:T(8,128)(2,1)S(1)}, bf16[2,8,2048]{2,1,0:T(8,128)(2,1)}, u32[]{:S(2)}) copy-start(bf16[2,8,2048]{2,1,0:T(8,128)(2,1)} %refs_2_.1) | copy-start | bytes 196612
